TPU v7x, 32 devices: a whole 2x2x4 slice. The times are simulated.
32 devices in a mesh: batch: 8 (over z, y), patch: 4 (over x, core).
Axes of the slice: x: 2, y: 2, z: 4, core: 2. Of those that a mesh axis runs over, the one named last changes fastest.
Arguments:
- tokens: bfloat16 [8, 8, 256, 1024], P('batch', None, 'patch'), may hold values from -6 to 6
- cotangent: bfloat16 [8, 8, 256, 1024], P('batch', None, 'patch'), may hold values from -6 to 6
- episode_frames: int32 [8, 4], P('batch'), may hold values from 1 to 4, 8 in all within a row
- kinds: int32 [8, 8, 256], P('batch', None, 'patch'), may hold values from 0 to 2, as said below
- patch_pos: int32 [8, 8, 256], P('batch', None, 'patch'), may hold values from 0 to 255, each once within a row
- ln1_gain: bfloat16 [1024], replicated, may hold values from 0.5 to 1.5
- ln1_shift: bfloat16 [1024], replicated, may hold values from -3 to 3
- w_qkv: bfloat16 [1024, 3072], replicated, may hold values from -0.1875 to 0.1875
- w_out: bfloat16 [1024, 1024], replicated, may hold values from -1.5 to 1.5
- ln2_gain: bfloat16 [1024], replicated, may hold values from 0.5 to 1.5
- ln2_shift: bfloat16 [1024], replicated, may hold values from -3 to 3
- w_up: bfloat16 [1024, 4096], replicated, may hold values from -0.1875 to 0.1875
- w_down: bfloat16 [4096, 1024], replicated, may hold values from -0.09375 to 0.09375
Outputs:
- out: bfloat16 [8, 8, 256, 1024], P('batch', None, 'patch')
- grad_tokens: bfloat16 [8, 8, 256, 1024], P('batch', None, 'patch')
- grad_ln1_gain: float32 [1024], P('patch')
- grad_ln1_shift: float32 [1024], P('patch')
- grad_w_qkv: float32 [1024, 3072], P('patch')
- grad_w_out: float32 [1024, 1024], P('patch')
- grad_ln2_gain: float32 [1024], P('patch')
- grad_ln2_shift: float32 [1024], P('patch')
- grad_w_up: float32 [1024, 4096], P('patch')
- grad_w_down: float32 [4096, 1024], P('patch')
Inputs may be any that keep to these rules, and one draw needn't show every extreme that they name: `episode_frames`: each group's 4 episodes have 1 or more frames, sum to 8, and the longest has exactly 4. `kinds`: in every frame exactly one slot holds 1 (action) and one holds 2 (state), both among the frame's first 64 slots; all other slots hold 0. `patch_pos`: each frame's values are a permutation of its slots' cells.
All inputs are finite; a program needn't handle non-finite values.
Results may differ from a plain program's by a relative error of at most 0.035.
Values may be sent and summed in bfloat16 or wider, within the bound.
No kernel may reach another device: no remote copies, remote signals or barrier semaphores. Data moves between devices by JAX's collectives and lax.ppermute only.
A program may use at most 320 MiB of HBM per device.

v0:
```python
import functools
import math

import jax
import jax.numpy as jnp
from jax import lax
from jax.experimental import pallas as pl
from jax.experimental.pallas import tpu as pltpu
from jax.sharding import PartitionSpec as P

GRID = 16
EPS = 1e-06
THETA = 10000.0
MASKED = -1e30
LIMIT = 48 * 1024 * 1024
BF = jnp.bfloat16
F32 = jnp.float32
AXES = ("batch", "patch")


def nn(a, b):
    return lax.dot_general(a, b, (((1,), (0,)), ((), ())), preferred_element_type=F32)


def nt(a, b):
    return lax.dot_general(a, b, (((1,), (1,)), ((), ())), preferred_element_type=F32)


def tn(a, b):
    return lax.dot_general(a, b, (((0,), (0,)), ((), ())), preferred_element_type=F32)


def params(*semantics):
    return pltpu.CompilerParams(
        dimension_semantics=semantics, vmem_limit_bytes=LIMIT
    )


def cost(flops, nbytes, trans=0):
    return pl.CostEstimate(flops=int(flops), bytes_accessed=int(nbytes), transcendentals=int(trans))


def full(shape, memory=None):
    zeros = (0,) * len(shape)
    return pl.BlockSpec(shape, lambda *_: zeros)


def blocked(ref, value):
    for n in range(ref.shape[0]):
        ref[n] = value[:, n * 128 : (n + 1) * 128].astype(BF)


def smem():
    return pl.BlockSpec(memory_space=pltpu.SMEM)


def normalise(x):
    mean = jnp.mean(x, axis=-1, keepdims=True)
    centred = x - mean
    spread = jnp.mean(centred * centred, axis=-1, keepdims=True)
    rstd = lax.rsqrt(spread + EPS)
    return centred * rstd, rstd


def norm_back(d_h, hat, rstd, gain):
    d_hat = d_h * gain
    first = jnp.mean(d_hat, axis=-1, keepdims=True)
    second = jnp.mean(d_hat * hat, axis=-1, keepdims=True)
    return rstd * (d_hat - first - hat * second)


def partner(value):
    head = 64
    half = head // 6
    width = value.shape[1]
    ahead = jnp.concatenate([value[:, half:], value[:, :half]], axis=1)
    behind = jnp.concatenate([value[:, width - half :], value[:, : width - half]], axis=1)
    lane = lax.broadcasted_iota(jnp.int32, value.shape, 1) % head
    return jnp.where(lane % (2 * half) < half, ahead, behind)


def widen(table, width):
    have = table.shape[1]
    if width <= have:
        return table[:, :width]
    return jnp.concatenate([table] * (width // have), axis=1)


def qkv_kernel(count, local, *refs):
    tok = refs[:count]
    cs_ref, w_ref, gain_ref, shift_ref = refs[count : count + 4]
    h_ref, qkv_ref = refs[count + 4 :]
    x = jnp.concatenate([t[...] for t in tok], axis=1)
    fb, rows, dim = x.shape
    x = x.reshape(fb * rows, dim).astype(F32)
    hat, _ = normalise(x)
    h = (hat * gain_ref[...] + shift_ref[...]).astype(BF)
    h_ref[...] = h.reshape(fb, rows, dim)
    y = nn(h, w_ref[...])
    cs = cs_ref[...].reshape(fb * rows, 256)
    cos = widen(cs[:, :128], local)
    sin = widen(cs[:, 128:], local)
    q = y[:, :local]
    k = y[:, local : 2 * local]
    q = (q * cos + partner(q) * sin).astype(BF) * BF(0.125)
    k = (k * cos + partner(k) * sin).astype(BF)
    qkv_ref[:, :, :local] = q.reshape(fb, rows, local)
    qkv_ref[:, :, local : 2 * local] = k.reshape(fb, rows, local)
    qkv_ref[:, :, 2 * local :] = y[:, 2 * local :].astype(BF).reshape(fb, rows, local)


def qkv_call(items, cs, w_local, gain, shift):
    count = len(items)
    frames, width, dim = items[0].shape
    local = w_local.shape[1] // 3
    rows = count * width
    fb = max(1, min(frames, 512 // rows))
    while frames % fb:
        fb -= 1
    shapes = [
        jax.ShapeDtypeStruct((frames, rows, dim), BF),
        jax.ShapeDtypeStruct((frames, rows, 3 * local), BF),
    ]
    return pl.pallas_call(
        functools.partial(qkv_kernel, count, local),
        grid=(frames // fb,),
        in_specs=[pl.BlockSpec((fb, width, dim), lambda i: (i, 0, 0))] * count
        + [
            pl.BlockSpec((fb, rows, 256), lambda i: (i, 0, 0)),
            full(w_local.shape),
            full(gain.shape),
            full(shift.shape),
        ],
        out_specs=[pl.BlockSpec((fb,) + s.shape[1:], lambda i: (i, 0, 0)) for s in shapes],
        out_shape=shapes,
        compiler_params=params("arbitrary"),
        cost_estimate=cost(
            2 * frames * rows * dim * 3 * local,
            frames * rows * (4 * dim + 1024 + 6 * local) + 6 * dim * local,
        ),
        name="qkv",
    )(*items, cs, w_local, gain, shift)


def lane_halves(shape):
    lane = lax.broadcasted_iota(jnp.int32, shape, 1)
    return lane < 64


def attend_kernel(groups, local, patches, most, info_ref, *refs):
    ins = refs[:groups]
    o_refs = refs[groups : groups + patches]
    of_ref, lse_ref = refs[groups + patches :]
    f = pl.program_id(0)
    begin = info_ref[1 + f]
    q = jnp.concatenate([r[f, :, :local] for r in ins], axis=0)
    rows = q.shape[0]
    low = lane_halves((rows, 128))
    one = jnp.ones((rows, 128), BF)
    zero = jnp.zeros((rows, 128), BF)
    lane = lax.broadcasted_iota(jnp.int32, (rows, 128), 1)

    def keys(g, at):
        return jnp.concatenate([r[g, :, at : at + 128] for r in ins], axis=0)

    def finish(pair, tops, accs, lses):
        num = jnp.where(low, accs[0], accs[1])
        den = pltpu.roll(jnp.where(low, accs[1], accs[0]), 64, 1)
        of_ref[0, :, pair * 128 : (pair + 1) * 128] = num / den
        logs = jnp.log(jnp.where(low, accs[1], accs[0]))
        lses = jnp.where(lane == 2 * pair + 64, tops[0] + logs, lses)
        return jnp.where(lane == 2 * pair + 1, tops[1] + logs, lses)

    def store(lses):
        even = lane % 2 == 0
        lses = jnp.where(even, pltpu.roll(lses, 64, 1), lses)
        lse_ref[0] = lses.T[:8]

    def whole(count):
        lses = jnp.zeros((rows, 128), F32)
        for pair in range(local // 128):
            at = pair * 128
            tops, accs = [], []
            for h in range(2):
                qm = jnp.where(low == (h == 0), q[:, at : at + 128], zero)
                scores = [nt(qm, keys(begin + n, local + at)) for n in range(count)]
                top = scores[0]
                for s in scores[1:]:
                    top = jnp.maximum(top, s)
                top = jnp.max(top, axis=1, keepdims=True)
                acc = None
                for n, s in enumerate(scores):
                    v = jnp.where(low == (h == 0), keys(begin + n, 2 * local + at), one)
                    part = nn(jnp.exp(s - top).astype(BF), v)
                    acc = part if acc is None else acc + part
                tops.append(top)
                accs.append(acc)
            lses = finish(pair, tops, accs, lses)
        store(lses)

    if most <= 4:
        for count in range(1, most + 1):
            pl.when(f + 1 - begin == count)(functools.partial(whole, count))
    else:
        lses = jnp.zeros((rows, 128), F32)
        for pair in range(local // 128):
            at = pair * 128

            def body(g, state):
                new = []
                for h in range(2):
                    top, acc = state[2 * h : 2 * h + 2]
                    qm = jnp.where(low == (h == 0), q[:, at : at + 128], zero)
                    s = nt(qm, keys(g, local + at))
                    new_top = jnp.maximum(top, jnp.max(s, axis=1, keepdims=True))
                    v = jnp.where(low == (h == 0), keys(g, 2 * local + at), one)
                    p = jnp.exp(s - new_top).astype(BF)
                    new += [new_top, acc * jnp.exp(top - new_top) + nn(p, v)]
                return tuple(new)

            blank = (jnp.full((rows, 1), MASKED, F32), jnp.zeros((rows, 128), F32))
            state = lax.fori_loop(begin, f + 1, body, blank + blank)
            lses = finish(pair, state[0::2], state[1::2], lses)
        store(lses)

    o = of_ref[0].astype(BF)
    width = rows // patches
    for j in range(patches):
        o_refs[j][0] = o[j * width : (j + 1) * width]


def attend_call(info, qkv, patches):
    groups = len(qkv)
    frames = qkv[0].shape[0]
    local = qkv[0].shape[2] // 3
    rows = sum(a.shape[1] for a in qkv)
    width = rows // patches
    shapes = [jax.ShapeDtypeStruct((frames, width, local), BF)] * patches
    shapes += [
        jax.ShapeDtypeStruct((frames, rows, local), F32),
        jax.ShapeDtypeStruct((frames, 8, rows), F32),
    ]
    return pl.pallas_call(
        functools.partial(attend_kernel, groups, local, patches, frames // 2),
        grid=(frames,),
        in_specs=[smem()] + [full(a.shape) for a in qkv],
        out_specs=[pl.BlockSpec((1,) + s.shape[1:], lambda i: (i, 0, 0)) for s in shapes],
        out_shape=shapes,
        compiler_params=params("arbitrary"),
        cost_estimate=cost(
            2 * 2 * 2 * frames * rows * rows * 2 * local, 14 * frames * rows * local
        ),
        name="attend",
    )(info, *qkv)


def attend_back_kernel(groups, local, patches, after, info_ref, *refs):
    refs = refs[after:]
    ins = refs[:groups]
    css = refs[groups : 2 * groups]
    do_refs = refs[2 * groups : 2 * groups + patches]
    refs = refs[2 * groups + patches :]
    of_ref, lse_ref = refs[:2]
    outs = refs[2 : groups + 2]
    dk_ref, dv_ref, dq_ref, kt_ref = refs[groups + 2 :]
    f = pl.program_id(0)
    frames = pl.num_programs(0)
    begin = info_ref[1 + f]
    q = jnp.concatenate([r[f, :, :local] for r in ins], axis=0)
    d_o = jnp.concatenate([r[0] for r in do_refs], axis=0)
    rows = q.shape[0]
    low = lane_halves((rows, 128))
    zero = jnp.zeros((rows, 128), BF)
    turned = (d_o.astype(F32) * of_ref[0]).T
    delta = [
        jnp.sum(turned[h * 64 : (h + 1) * 64], axis=0, keepdims=True) for h in range(local // 64)
    ]
    lse = lse_ref[0]
    dk_ref[f] = jnp.zeros((rows, local), F32)
    dv_ref[f] = jnp.zeros((rows, local), F32)
    dq_ref[...] = jnp.zeros((local, rows), F32)
    kt_ref[f] = jnp.concatenate([r[f, :, local : 2 * local] for r in ins], axis=0).T

    def masked(a):
        return [
            [jnp.where(low == (h == 0), a[:, at : at + 128], zero) for h in range(2)]
            for at in range(0, local, 128)
        ]

    qm = masked(q)
    dom = masked(d_o)

    @pl.loop(begin, f + 1)
    def _(g):
        for pair in range(local // 128):
            at = pair * 128
            k = jnp.concatenate([r[g, :, local + at : local + at + 128] for r in ins], axis=0)
            v = jnp.concatenate(
                [r[g, :, 2 * local + at : 2 * local + at + 128] for r in ins], axis=0
            )
            dk = dv = None
            for h in range(2):
                head = 2 * pair + h
                p = jnp.exp(nt(k, qm[pair][h]) - lse[head : head + 1])
                dp = nt(v, dom[pair][h])
                ds = (p * (dp - delta[head])).astype(BF)
                dq_ref[head * 64 : (head + 1) * 64] += nn(
                    kt_ref[g, head * 64 : (head + 1) * 64], ds
                )
                part_k = nn(ds, qm[pair][h])
                part_v = nn(p.astype(BF), dom[pair][h])
                dk = part_k if dk is None else dk + part_k
                dv = part_v if dv is None else dv + part_v
            dk_ref[g, :, at : at + 128] += dk
            dv_ref[g, :, at : at + 128] += dv

    def tables(t):
        cs = jnp.concatenate([r[t] for r in css], axis=0)
        return widen(cs[:, :128], local), widen(cs[:, 128:], local)

    def put(t, at, value):
        start = 0
        for out in outs:
            n = out.shape[1]
            out[t, :, at * local : (at + 1) * local] = value[start : start + n]
            start += n

    cos, sin = tables(f)
    dq = dq_ref[...].T * 0.125
    put(f, 0, (dq * cos - partner(dq) * sin).astype(BF))

    @pl.when(f == frames - 1)
    def _():
        @pl.loop(0, frames)
        def _(t):
            cos, sin = tables(t)
            dk = dk_ref[t]
            put(t, 1, (dk * cos - partner(dk) * sin).astype(BF))
            put(t, 2, dv_ref[t].astype(BF))


def attend_back_call(info, qkv, cs, d_o, o_full, lse, patches, after=()):
    groups = len(qkv)
    frames = qkv[0].shape[0]
    local = qkv[0].shape[2] // 3
    rows = sum(a.shape[1] for a in qkv)
    width = rows // patches
    shapes = [jax.ShapeDtypeStruct((frames, a.shape[1], 3 * local), BF) for a in qkv]
    return pl.pallas_call(
        functools.partial(attend_back_kernel, groups, local, patches, len(after)),
        grid=(frames,),
        in_specs=[smem()]
        + [pl.BlockSpec(memory_space=pl.ANY)] * len(after)
        + [full(a.shape) for a in qkv]
        + [full(a.shape) for a in cs]
        + [pl.BlockSpec((1, width, local), lambda i: (i, 0, 0))] * patches
        + [
            pl.BlockSpec((1, rows, local), lambda i: (i, 0, 0)),
            pl.BlockSpec((1, 8, rows), lambda i: (i, 0, 0)),
        ],
        out_specs=[full(s.shape) for s in shapes],
        out_shape=shapes,
        scratch_shapes=[
            pltpu.VMEM((frames, rows, local), F32),
            pltpu.VMEM((frames, rows, local), F32),
            pltpu.VMEM((local, rows), F32),
            pltpu.VMEM((frames, local, rows), BF),
        ],
        compiler_params=params("arbitrary"),
        cost_estimate=cost(
            5 * 2 * 2 * frames * rows * rows * 2 * local, 20 * frames * rows * local
        ),
        name="attend_back",
    )(info, *after, *qkv, *cs, *d_o, o_full, lse)


def heads_rows(info_ref, j, local):
    return pl.ds(pl.multiple_of((info_ref[0] ^ j) * local, local), local)


def project_kernel(patches, info_ref, *refs):
    o_refs = refs[:patches]
    x_ref, w_ref, gain_ref, shift_ref, x1_ref, h_ref = refs[patches:]
    fb, width, local = o_refs[0].shape
    rows = fb * width
    acc = x_ref[...].astype(F32).reshape(rows, -1)
    for j, o_ref in enumerate(o_refs):
        acc = acc + nn(o_ref[...].reshape(rows, local), w_ref[heads_rows(info_ref, j, local), :])
    x1_ref[...] = acc
    hat, _ = normalise(acc)
    h_ref[...] = (hat * gain_ref[...] + shift_ref[...]).astype(BF)


def project_call(info, o_in, tokens, w_out, gain, shift):
    patches = len(o_in)
    frames, width, local = o_in[0].shape
    dim = w_out.shape[0]
    fb = frames // 2
    rows = frames * width
    return pl.pallas_call(
        functools.partial(project_kernel, patches),
        grid=(2,),
        in_specs=[smem()]
        + [pl.BlockSpec((fb, width, local), lambda i: (i, 0, 0))] * patches
        + [
            pl.BlockSpec((fb, width, dim), lambda i: (i, 0, 0)),
            full(w_out.shape),
            full(gain.shape),
            full(shift.shape),
        ],
        out_specs=[
            pl.BlockSpec((rows // 2, dim), lambda i: (i, 0)),
            pl.BlockSpec((rows // 2, dim), lambda i: (i, 0)),
        ],
        out_shape=[
            jax.ShapeDtypeStruct((rows, dim), F32),
            jax.ShapeDtypeStruct((rows, dim), BF),
        ],
        compiler_params=params("arbitrary"),
        cost_estimate=cost(2 * rows * dim * dim, rows * dim * 10 + 2 * dim * dim),
        name="project",
    )(info, *o_in, tokens, w_out, gain, shift)


def hidden_block(hidden, patches):
    tile = min(256, hidden // patches)
    per = hidden // patches // tile

    def at(i, info):
        return ((i // per) * 2 + (info[0] & 1)) * per + i % per

    return tile, per, hidden // 2 // tile, at


def pre_kernel(info_ref, dy_own, dy_mate, down_ref, dg_ref):
    half = dy_own.shape[0]
    dg_ref[:half] = nt(dy_own[...], down_ref[...]).astype(BF)
    dg_ref[half:] = nt(dy_mate[...], down_ref[...]).astype(BF)


def pre_call(info, dy_own, dy_mate, w_down, patches):
    half, dim = dy_own.shape
    hidden = w_down.shape[0]
    tile, _, steps, at = hidden_block(hidden, patches)
    return pl.pallas_call(
        pre_kernel,
        grid_spec=pltpu.PrefetchScalarGridSpec(
            num_scalar_prefetch=1,
            grid=(steps,),
            in_specs=[full((half, dim))] * 2
            + [pl.BlockSpec((tile, dim), lambda i, info: (at(i, info), 0))],
            out_specs=pl.BlockSpec((2 * half, tile), lambda i, info: (0, i)),
        ),
        out_shape=jax.ShapeDtypeStruct((2 * half, hidden // 2), BF),
        compiler_params=params("arbitrary"),
        cost_estimate=cost(2 * half * dim * hidden, 6 * dim * hidden // 2),
        name="pre",
    )(info, dy_own, dy_mate, w_down)


def ffn_kernel(
    info_ref, h_own, h_mate, dy_own, dy_mate, dg_ref, up_ref,
    g_ref, du_ref, dh_own, dh_mate, dw_ref, acc_ref,
):
    step = pl.program_id(0)
    w_up = up_ref[...]
    half = h_own.shape[0]
    total = None
    for n, (h_ref, dy_ref) in enumerate(((h_own, dy_own), (h_mate, dy_mate))):
        rows = slice(n * half, (n + 1) * half)
        u = nn(h_ref[...], w_up)
        cdf = 0.5 + 0.5 * lax.erf(u * math.sqrt(0.5))
        pdf = jnp.exp(u * u * -0.5) * (1.0 / math.sqrt(2.0 * math.pi))
        g = (u * cdf).astype(BF)
        du = (dg_ref[rows].astype(F32) * (cdf + u * pdf)).astype(BF)
        g_ref[rows] = g
        du_ref[rows] = du
        part = nt(du, w_up)

        @pl.when(step == 0)
        def _():
            acc_ref[rows] = part

        @pl.when(step > 0)
        def _():
            acc_ref[rows] += part

        dw = tn(g, dy_ref[...])
        total = dw if total is None else total + dw
    blocked(dw_ref, total)

    @pl.when(step == pl.num_programs(0) - 1)
    def _():
        dh_own[...] = acc_ref[:half]
        dh_mate[...] = acc_ref[half:].astype(BF)


def ffn_call(info, h_own, h_mate, dy_own, dy_mate, dg, w_up, patches):
    half, dim = h_own.shape
    hidden = w_up.shape[1]
    tile, _, steps, at = hidden_block(hidden, patches)
    column = pl.BlockSpec((2 * half, tile), lambda i, info: (0, i))
    grid_spec = pltpu.PrefetchScalarGridSpec(
        num_scalar_prefetch=1,
        grid=(steps,),
        in_specs=[full((half, dim))] * 4
        + [column, pl.BlockSpec((dim, tile), lambda i, info: (0, at(i, info)))],
        out_specs=[
            column,
            column,
            full((half, dim)),
            full((half, dim)),
            pl.BlockSpec((dim // 128, tile, 128), lambda i, info: (0, i, 0)),
        ],
        scratch_shapes=[pltpu.VMEM((2 * half, dim), F32)],
    )
    return pl.pallas_call(
        ffn_kernel,
        grid_spec=grid_spec,
        out_shape=[
            jax.ShapeDtypeStruct((2 * half, hidden // 2), BF),
            jax.ShapeDtypeStruct((2 * half, hidden // 2), BF),
            jax.ShapeDtypeStruct((half, dim), F32),
            jax.ShapeDtypeStruct((half, dim), BF),
            jax.ShapeDtypeStruct((dim // 128, hidden // 2, 128), BF),
        ],
        compiler_params=params("arbitrary"),
        cost_estimate=cost(6 * 2 * half * dim * hidden // 2, 4 * dim * hidden),
        name="ffn",
    )(info, h_own, h_mate, dy_own, dy_mate, dg, w_up)


def ffn_rest_kernel(
    info_ref, h_own, h_mate, x1_ref, g_ref, du_ref, down_ref,
    dw_ref, out_own, out_mate, ht_ref, acc_ref,
):
    step = pl.program_id(0)
    half = h_own.shape[0]

    @pl.when(step == 0)
    def _():
        ht_ref[:, :half] = h_own[...].T
        ht_ref[:, half:] = h_mate[...].T
        acc_ref[:half] = x1_ref[...]
        acc_ref[half:] = jnp.zeros_like(x1_ref)

    blocked(dw_ref, nn(ht_ref[...], du_ref[...]))
    for n in range(2):
        rows = slice(n * half, (n + 1) * half)
        acc_ref[rows] += nn(g_ref[rows], down_ref[...])

    @pl.when(step == pl.num_programs(0) - 1)
    def _():
        out_own[...] = acc_ref[:half]
        out_mate[...] = acc_ref[half:].astype(BF)


def ffn_rest_call(info, h_own, h_mate, x1, g, du, w_down, patches):
    half, dim = h_own.shape
    hidden = w_down.shape[0]
    tile, per, steps, at = hidden_block(hidden, patches)
    grid_spec = pltpu.PrefetchScalarGridSpec(
        num_scalar_prefetch=1,
        grid=(steps,),
        in_specs=[full((half, dim))] * 3
        + [
            pl.BlockSpec((2 * half, tile), lambda i, info: (0, i)),
            pl.BlockSpec((2 * half, tile), lambda i, info: (0, i)),
            pl.BlockSpec((tile, dim), lambda i, info: (at(i, info), 0)),
        ],
        out_specs=[
            pl.BlockSpec((tile // 128, dim, 128), lambda i, info: (i, 0, 0)),
            full((half, dim)),
            full((half, dim)),
        ],
        scratch_shapes=[pltpu.VMEM((dim, 2 * half), BF), pltpu.VMEM((2 * half, dim), F32)],
    )
    return pl.pallas_call(
        ffn_rest_kernel,
        grid_spec=grid_spec,
        out_shape=[
            jax.ShapeDtypeStruct((hidden // 256, dim, 128), BF),
            jax.ShapeDtypeStruct((half, dim), F32),
            jax.ShapeDtypeStruct((half, dim), BF),
        ],
        compiler_params=params("arbitrary"),
        cost_estimate=cost(4 * 2 * half * dim * hidden // 2, 6 * dim * hidden),
        name="ffn_rest",
    )(info, h_own, h_mate, x1, g, du, w_down)


def mid_kernel(
    patches, info_ref, dh_ref, recv_ref, x1_ref, dy_ref, w_ref, gain_ref, dx_ref, da_ref, gs_ref,
    *do_refs,
):
    step = pl.program_id(0)
    fb, width, local = do_refs[0].shape
    hat, rstd = normalise(x1_ref[...])
    dh = dh_ref[...] + recv_ref[...].astype(F32)
    dx = dy_ref[...].astype(F32) + norm_back(dh, hat, rstd, gain_ref[...])
    dx_ref[...] = dx
    da = dx.astype(BF)
    da_ref[...] = da
    sums = jnp.concatenate(
        [jnp.sum(dh * hat, axis=0, keepdims=True), jnp.sum(dh, axis=0, keepdims=True)], axis=0
    )

    @pl.when(step == 0)
    def _():
        gs_ref[...] = sums

    @pl.when(step > 0)
    def _():
        gs_ref[...] += sums

    for j, do_ref in enumerate(do_refs):
        part = nt(da, w_ref[heads_rows(info_ref, j, local), :])
        do_ref[...] = part.astype(BF).reshape(fb, width, local)


def mid_call(info, dh, recv, x1, dy, w_out, gain, frames, patches):
    rows, dim = x1.shape
    width = rows // frames
    local = dim // patches
    fb = frames // 2
    row = pl.BlockSpec((rows // 2, dim), lambda i: (i, 0))
    return pl.pallas_call(
        functools.partial(mid_kernel, patches),
        grid=(2,),
        in_specs=[smem(), row, row, row, row, full(w_out.shape), full(gain.shape)],
        out_specs=[row, row, full((2, dim))]
        + [pl.BlockSpec((fb, width, local), lambda i: (i, 0, 0))] * patches,
        out_shape=[
            jax.ShapeDtypeStruct((rows, dim), F32),
            jax.ShapeDtypeStruct((rows, dim), BF),
            jax.ShapeDtypeStruct((2, dim), F32),
        ]
        + [jax.ShapeDtypeStruct((frames, width, local), BF)] * patches,
        compiler_params=params("arbitrary"),
        cost_estimate=cost(2 * rows * dim * dim, rows * dim * 20 + 2 * dim * dim),
        name="mid",
    )(info, dh, recv, x1, dy, w_out, gain)


def dwo_kernel(patches, info_ref, *refs):
    o_refs, da_ref, dw_ref = refs[:patches], refs[patches], refs[patches + 1]
    frames, width, local = o_refs[0].shape
    for j, o_ref in enumerate(o_refs):
        part = tn(o_ref[...].reshape(frames * width, local), da_ref[...]).astype(BF)
        at = heads_rows(info_ref, j, local)
        for n in range(dw_ref.shape[0]):
            dw_ref[n, at, :] = part[:, n * 128 : (n + 1) * 128]


def dwo_call(info, o_in, da):
    patches = len(o_in)
    dim = da.shape[1]
    shape = (dim // 128, dim, 128)
    return pl.pallas_call(
        functools.partial(dwo_kernel, patches),
        grid=(1,),
        in_specs=[smem()] + [full(a.shape) for a in o_in] + [full(da.shape)],
        out_specs=full(shape),
        out_shape=jax.ShapeDtypeStruct(shape, BF),
        compiler_params=params("arbitrary"),
        cost_estimate=cost(2 * da.shape[0] * dim * dim, 6 * dim * dim),
        name="dwo",
    )(info, *o_in, da)


def dqkv_kernel(groups, *refs):
    hs = refs[:groups]
    ds = refs[groups : 2 * groups]
    w_ref = refs[2 * groups]
    dh = refs[2 * groups + 1 : 3 * groups + 1]
    dw_ref = refs[3 * groups + 1]
    acc_ref = refs[3 * groups + 2]
    step = pl.program_id(0)
    total = None
    for h_ref, d_ref, out in zip(hs, ds, dh):
        fb, rows, dim = h_ref.shape
        d = d_ref[...].reshape(fb * rows, -1)
        out[...] = nt(d, w_ref[...]).astype(BF).reshape(fb, rows, dim)
        part = tn(h_ref[...].reshape(fb * rows, dim), d)
        total = part if total is None else total + part

    @pl.when(step == 0)
    def _():
        acc_ref[...] = total

    @pl.when(step > 0)
    def _():
        acc_ref[...] += total

    @pl.when(step == pl.num_programs(0) - 1)
    def _():
        blocked(dw_ref, acc_ref)


def dqkv_call(hs, ds, w_local):
    groups = len(hs)
    frames = hs[0].shape[0]
    dim, cols = w_local.shape
    rows = sum(a.shape[1] for a in hs)
    fb = max(1, min(frames, 512 // rows))

    def blocks(a):
        return pl.BlockSpec((fb,) + a.shape[1:], lambda i: (i, 0, 0))

    shapes = [jax.ShapeDtypeStruct(a.shape, BF) for a in hs]
    shapes.append(jax.ShapeDtypeStruct((cols // 128, dim, 128), BF))
    return pl.pallas_call(
        functools.partial(dqkv_kernel, groups),
        grid=(frames // fb,),
        in_specs=[blocks(a) for a in hs] + [blocks(a) for a in ds] + [full(w_local.shape)],
        out_specs=[blocks(a) for a in hs] + [full((cols // 128, dim, 128))],
        out_shape=shapes,
        scratch_shapes=[pltpu.VMEM((dim, cols), F32)],
        compiler_params=params("arbitrary"),
        cost_estimate=cost(4 * frames * rows * dim * cols, frames * rows * 4 * dim),
        name="dqkv",
    )(*hs, *ds, w_local)


def last_kernel(a_ref, b_ref, x_ref, dx_ref, gain_ref, gt_ref, gs_ref):
    step = pl.program_id(0)
    hat, rstd = normalise(x_ref[...].astype(F32))
    dh = a_ref[...].astype(F32) + b_ref[...].astype(F32)
    gt_ref[...] = (dx_ref[...] + norm_back(dh, hat, rstd, gain_ref[...])).astype(BF)
    sums = jnp.concatenate(
        [jnp.sum(dh * hat, axis=0, keepdims=True), jnp.sum(dh, axis=0, keepdims=True)], axis=0
    )

    @pl.when(step == 0)
    def _():
        gs_ref[...] = sums

    @pl.when(step > 0)
    def _():
        gs_ref[...] += sums


def last_call(a, b, x, dx, gain):
    rows, dim = x.shape
    row = pl.BlockSpec((rows // 2, dim), lambda i: (i, 0))
    return pl.pallas_call(
        last_kernel,
        grid=(2,),
        in_specs=[row, row, row, row, full(gain.shape)],
        out_specs=[row, full((2, dim))],
        out_shape=[
            jax.ShapeDtypeStruct((rows, dim), BF),
            jax.ShapeDtypeStruct((2, dim), F32),
        ],
        compiler_params=params("arbitrary"),
        cost_estimate=cost(40 * rows * dim, rows * dim * 12),
        name="last",
    )(a, b, x, dx, gain)


class Chain:
    def __init__(self, hops):
        self.hops, self.value, self.got, self.begun, self.done = hops, None, None, False, False

    def request(self):
        try:
            return self.hops.send(self.got) if self.begun else next(self.hops)
        except StopIteration as stop:
            self.value, self.done = stop.value, True
            return None
        finally:
            self.begun = True


class Stage:
    def __init__(self, links):
        self.links, self.moves = links, []

    def step(self, *chains):
        wanted = {}
        for chain in chains:
            if chain.done:
                continue
            request = chain.request()
            if request is not None:
                wanted.setdefault(request[0], []).append((chain, request[1]))
        for bit, members in wanted.items():
            arrays = [a for _, a in members]
            if bit == "patch":
                sent = arrays[0] if len(arrays) == 1 else jnp.concatenate(arrays, axis=0)
                got = lax.all_to_all(sent, "patch", 1, 1, tiled=True)
            elif len(arrays) == 1:
                got = self.links.swap(arrays[0], bit)
            else:
                sent = jnp.concatenate([a.reshape(-1, 128) for a in arrays], axis=0)
                got = self.links.swap(sent, bit)
            self.moves.append((bit, members, got))

    def close(self, values):
        held, values = lax.optimization_barrier(([m[2] for m in self.moves], values))
        for (bit, members, _), got in zip(self.moves, held):
            start = 0
            for chain, a in members:
                if len(members) == 1:
                    chain.got = got
                elif bit == "patch":
                    chain.got = got[start : start + a.shape[0]]
                    start += a.shape[0]
                else:
                    n = a.size // 128
                    chain.got = got[start : start + n].reshape(a.shape)
                    start += n
        self.moves = []
        return values


class Links:
    def __init__(self, batches, patches):
        self.batches, self.patches = batches, patches
        self.patch = lax.axis_index("patch")
        self.batch = lax.axis_index("batch")
        self.bits = {"c": [("p", 1)], "y": [("b", 1)], "x": [], "z": []}
        bit = 2
        while bit < patches:
            self.bits["x"].append(("p", bit))
            bit *= 2
        bit = 2
        while bit < batches:
            self.bits["z"].append(("b", bit))
            bit *= 2

    def swap(self, a, bit):
        axis, step = bit
        step = step if axis == "p" else step * self.patches
        n = self.batches * self.patches
        return lax.ppermute(a, AXES, [(i, i ^ step) for i in range(n)])

    def swap_patch(self, a, bit):
        return self.swap(a, ("p", bit))

    def mine(self, bit):
        axis, step = bit
        return ((self.patch if axis == "p" else self.batch) // step) & 1

    def expand(self, order):
        bits = []
        for axis in order:
            one = self.bits[axis.lower()]
            bits += one if axis.islower() else one[::-1]
        return bits

    def hops(self, a, axes, order, back, trade):
        names = self.expand(axes)
        blocks, rows, _ = a.shape
        a = a.reshape((blocks,) + (2,) * len(names) + (rows // 2 ** len(names), 128))
        layout = [bit for bit in names if bit[0] == "b"]
        for bit in self.expand(order):
            at = names.index(bit) + 1
            names.pop(at - 1)
            got = yield bit, lax.dynamic_index_in_dim(a, 1 - self.mine(bit), at, keepdims=False)
            keep = lax.dynamic_index_in_dim(a, self.mine(bit), at, keepdims=False)
            a = (keep.astype(F32) + got.astype(F32)).astype(BF)
        if trade == "core":
            bit = ("p", 1)
            got = yield bit, lax.dynamic_index_in_dim(a, 1 - self.mine(bit), 1, keepdims=False)
            own = lax.dynamic_index_in_dim(a, self.mine(bit), 1, keepdims=False)
            a = self.join(own, got, bit, 0)
            a = a.reshape((2 * blocks,) + a.shape[2:])
        if trade == "patch":
            a = a.reshape((blocks, self.patches) + a.shape[-2:])
            a = yield "patch", a
            a = a.reshape((blocks * self.patches,) + a.shape[-2:])
        have = []
        for bit in self.expand(back):
            got = yield bit, a
            at = 1 + sum(layout.index(other) < layout.index(bit) for other in have)
            have.append(bit)
            a = self.join(a, got, bit, at)
        return a.reshape(a.shape[0], -1, 128)

    def join(self, a, got, bit, at):
        return jnp.where(
            self.mine(bit) == 0, jnp.stack([a, got], axis=at), jnp.stack([got, a], axis=at)
        )

    def chain(self, a, axes, order, back, trade=None):
        return Chain(self.hops(a, axes, order, back, trade))

    def apart(self, a):
        got = {0: a}
        bit = self.patches // 2
        while bit > 1:
            for j in sorted(got):
                got[j | bit] = self.swap_patch(got[j], bit)
            bit //= 2
        return got

    def items(self, a):
        got = self.apart(a)
        for j in sorted(got):
            got[j | 1] = self.swap_patch(got[j], 1)
        return got

    def deal(self, parts):
        return [parts[0]] + [self.swap_patch(parts[j], j) for j in range(1, self.patches)]


def assemble_kernel(count, order, valid, *refs):
    out = refs[count]
    pieces = [refs[n][b][:, :valid].astype(F32) for n, b in order]
    out[...] = jnp.concatenate(pieces, axis=1)


def assemble(parts, order, valid=128):
    rows = parts[0].shape[1]
    step = min(rows, 128)
    return pl.pallas_call(
        functools.partial(assemble_kernel, len(parts), order, valid),
        grid=(rows // step,),
        in_specs=[pl.BlockSpec((a.shape[0], step, 128), lambda i: (0, i, 0)) for a in parts],
        out_specs=pl.BlockSpec((step, len(order) * valid), lambda i: (i, 0)),
        out_shape=jax.ShapeDtypeStruct((rows, len(order) * valid), F32),
        compiler_params=params("arbitrary"),
        cost_estimate=cost(0, 6 * rows * len(order) * 128),
        name="assemble",
    )(*parts)


def tables(code, times):
    head = 64
    half = head // 6
    band = 2 * half
    dims = jnp.arange(head)
    freq = jnp.power(THETA, -2.0 * (dims % half).astype(F32) / band)
    places = jnp.stack([times, (code // GRID).astype(F32), (code % GRID).astype(F32)], axis=-1)
    which = jnp.minimum(dims // band, 2)
    pick = jnp.where(
        which == 0, places[..., 0:1], jnp.where(which == 1, places[..., 1:2], places[..., 2:3])
    )
    angle = pick * freq
    turned = dims < 3 * band
    cos = jnp.where(turned, jnp.cos(angle), 1.0)
    sin = jnp.where(turned, jnp.sin(angle) * jnp.where(dims % band < half, -1.0, 1.0), 0.0)
    return jnp.concatenate([cos, cos, sin, sin], axis=-1)


def per_device(
    batches, patches, tokens, cotangent, episode_frames, kinds, patch_pos,
    ln1_gain, ln1_shift, w_qkv, w_out, ln2_gain, ln2_shift, w_up, w_down,
):
    tokens = tokens[0]
    frames, width, dim = tokens.shape
    rows = frames * width
    local = dim // patches
    links = Links(batches, patches)
    me = links.patch
    core = me & 1
    gain1, shift1, gain2, shift2 = (
        a.astype(F32).reshape(1, dim) for a in (ln1_gain, ln1_shift, ln2_gain, ln2_shift)
    )
    dy = cotangent.reshape(rows, dim)

    code = jnp.where(kinds[0] == 0, patch_pos[0], 0)
    codes = links.items(code)
    codes, tokens, dy = lax.optimization_barrier((codes, tokens, dy))
    mate = links.swap_patch(tokens, 1)
    dy_mate = links.swap_patch(dy, 1)
    apart = links.apart(tokens)
    ends = jnp.cumsum(episode_frames[0])
    frame_ids = jnp.arange(frames, dtype=jnp.int32)
    starts = jnp.max(
        jnp.where(ends[None, :] <= frame_ids[:, None], ends[None, :], 0), axis=1
    )
    info = jnp.concatenate([me[None], starts]).astype(jnp.int32)
    pad = max(128, local)
    columns = []
    for n in range(3):
        columns.append(
            lax.dynamic_slice(w_qkv, (jnp.int32(0), n * dim + me * local), (dim, local))
        )
        if pad > local:
            columns.append(jnp.zeros((dim, pad - local), BF))
    w_local = jnp.concatenate(columns, axis=1)

    members = [[0, 1], list(range(2, patches))]
    css = []
    for group in members:
        place = jnp.concatenate([codes[j] for j in group], axis=1)
        times = jnp.broadcast_to(frame_ids.astype(F32)[:, None], place.shape)
        css.append(tables(place, times))
    near = qkv_call([tokens, mate], css[0], w_local, gain1, shift1)
    dg = pre_call(info, dy, dy_mate, w_down, patches)
    near, dg, apart, css = lax.optimization_barrier((near, dg, apart, css))
    far_items = []
    for j in range(2, patches, 2):
        far_items += [apart[j], links.swap_patch(apart[j], 1)]
    far = qkv_call(far_items, css[1], w_local, gain1, shift1)
    hs, qkvs = [near[0], far[0]], [near[1], far[1]]

    *o_send, o_full, lse = attend_call(info, qkvs, patches)
    o_in = links.deal([a[..., :local] for a in o_send])
    x1, h2 = project_call(info, o_in, tokens, w_out, gain2, shift2)
    h2_mate = links.swap_patch(h2, 1)
    g, du, dh_own, dh_mate, dw_down = ffn_call(
        info, h2, h2_mate, dy, dy_mate, dg, w_up, patches
    )
    dh_recv = links.swap_patch(dh_mate, 1)

    stage = Stage(links)
    half = dim // 256
    d1 = links.chain(dw_down[:half], "Xyz", "yzx", "Zy")
    d2 = links.chain(dw_down[half:], "Xyz", "zxy", "yZ")
    stage.step(d1, d2)
    dx1, da, sums2, *d_o = mid_call(
        info, dh_own, dh_recv, x1, dy, w_out, gain2, frames, patches
    )
    d_o, g, da = lax.optimization_barrier((d_o, g, da))
    do_in = links.deal(d_o)
    dw_up, out_own, out_mate = ffn_rest_call(info, h2, h2_mate, x1, g, du, w_down, patches)
    out_recv = links.swap_patch(out_mate, 1)
    dw_out = dwo_call(info, o_in, da)
    do_in, dw_up, dw_out, out_own, out_recv = stage.close(
        (do_in, dw_up, dw_out, out_own, out_recv)
    )
    out = (out_own + out_recv.astype(F32)).astype(BF)

    half = dw_up.shape[0] // 2
    u1 = links.chain(dw_up[:half], "Xcyz", "xyz", "Zy", "core")
    u2 = links.chain(dw_up[half:], "Xcyz", "yzx", "yZ", "core")
    wo = links.chain(dw_out, "Xcyz", "cxyz", "Zy")
    stage.step(d1, d2, u1, u2, wo)
    if pad > local:
        do_in = [jnp.pad(a, ((0, 0), (0, 0), (0, pad - local))) for a in do_in]
    dqkv = attend_back_call(info, qkvs, css, do_in, o_full, lse, patches)
    dqkv = stage.close(dqkv)

    stage.step(d1, d2, u1, u2)
    *dh1, dw_qkv = dqkv_call(hs, dqkv, w_local)
    dh1, dw_qkv = stage.close((dh1, dw_qkv))

    slots = []
    for group, part in zip(members, dh1):
        part = part.reshape(frames, len(group), width, dim)
        slots += [part[:, n] for n in range(len(group))]
    even = jnp.stack(slots[0::2])
    odd = links.swap_patch(jnp.stack(slots[1::2]), 1)
    half = dw_qkv.shape[0] // 2
    q1 = links.chain(dw_qkv[:half], "Xcyz", "yz", "Zy", "patch")
    q2 = links.chain(dw_qkv[half:], "Xcyz", "zy", "yZ", "patch")
    stage.step(q1, q2, d1, d2, u1, u2, wo)
    odd, even = stage.close((odd, even))
    slots = (even.astype(F32) + odd.astype(F32)).astype(BF)
    bit = patches // 2
    while bit > 2:
        n = slots.shape[0] // 2
        slots = (slots[:n].astype(F32) + links.swap_patch(slots[n:], bit).astype(F32)).astype(BF)
        bit //= 2
    got = links.swap_patch(slots[1], 2)
    stage.step(q1, q2, d1, d2, u1, wo)
    slots, got = stage.close((slots, got))
    stage.step(q1, q2, d1, d2, u1, u2, wo)
    grad_tokens, sums1 = last_call(
        slots[0].reshape(rows, dim), got.reshape(rows, dim), tokens.reshape(rows, dim), dx1, gain1
    )
    sums = jnp.concatenate([sums1, sums2], axis=0)
    sums = sums.reshape(4, patches, local).transpose(1, 0, 2)
    grad_tokens, sums = stage.close((grad_tokens, sums))
    stage.step(q1, q2, d1, d2, u1, u2, wo)
    sums = lax.all_to_all(sums, "patch", 0, 0, tiled=True)
    sums = stage.close(sums)
    stage.step(q1, q2, d1, d2, u1, u2, wo)
    sums = jnp.sum(sums, axis=0)
    sums = jnp.broadcast_to(sums[None], (batches,) + sums.shape)
    sums = lax.all_to_all(sums, "batch", 0, 0, tiled=True)
    sums = stage.close(sums)
    sums = jnp.sum(sums, axis=0)
    chains = (q1, q2, d1, d2, u1, u2, wo)
    while not all(c.done for c in chains):
        stage.step(*chains)
        sums = stage.close(sums)

    nx = patches // 2
    half = dim // 256
    down = assemble(
        [d1.value, d2.value], [(n, b) for n in range(2) for b in range(half)]
    )
    per = w_up.shape[1] // patches // 128
    half = u1.value.shape[0] // 2
    order = []
    for i in range(nx):
        for owner in range(2):
            for t in range(per):
                b = i * per + t
                order.append((0, owner * half + b) if b < half else (1, owner * half + b - half))
    up = assemble([u1.value, u2.value], order)
    grad_wo = assemble([wo.value], [(0, b) for b in range(dim // 128)])
    order = []
    half = dw_qkv.shape[0] // 2
    for n in range(3):
        for p in range(patches):
            for t in range(pad // 128):
                b = n * (pad // 128) + t
                order.append((0, b * patches + p) if b < half else (1, (b - half) * patches + p))
    qkv = assemble([q1.value, q2.value], order, min(128, local))

    return (
        out.reshape(1, frames, width, dim),
        grad_tokens.reshape(1, frames, width, dim),
        sums[0],
        sums[1],
        qkv,
        grad_wo,
        sums[2],
        sums[3],
        up,
        down,
    )


def solution(mesh):
    placed = (
        P("batch", None, "patch", None),
        P("batch", None, "patch", None),
        P("batch", None),
        P("batch", None, "patch"),
        P("batch", None, "patch"),
    ) + (P(),) * 8
    return jax.shard_map(
        functools.partial(per_device, mesh.shape["batch"], mesh.shape["patch"]),
        mesh=mesh,
        in_specs=placed,
        out_specs=(
            P("batch", None, "patch", None),
            P("batch", None, "patch", None),
            P("patch"),
            P("patch"),
            P("patch", None),
            P("patch", None),
            P("patch"),
            P("patch"),
            P("patch", None),
            P("patch", None),
        ),
        check_vma=False,
    )
```

profile of v0, /device:TPU:0, one launch (start us, length us, event | category | flops | bytes accessed | tf_op | source)
XLA Modules:
  0.0 414.3 jit_solution(14345192542948999200)
XLA Ops:
  12.9 3.9 cosine_select_fusion.1
  17.8 6.2 %qkv.2 = (bf16[8,128,1024]{2,1,0:T(8,128)(2,1)}, bf16[8,128,768]{2,1,0:T(8,128)(2,1)S(1)}) custom-call(bf16[8,64,1024]{2,1,0:T(8,128)(2,1)S(1)} %bitcast.326, bf16[8,64,1024]{2,1,0:T(8,128)(2,1)S(1)} %collective-permute-done.3.refs_1_, f32[8,128,256]{2,1,0:T(8,128)S(1)} %pad_maximum_fusion.3.refs_2_, bf16[1024,768]{1,0:T(8,128)(2,1)} %pad_maximum_fusion.2.refs_3_.refs_4_, ...), custom_call_target="tpu_custom_call" | custom-call | flops 1610612736 | bytes 8388608 | tf_op jit(solution)/shard_map/qkv/pallas_call | solution.py:124
  24.0 10.0 %pre.1.dg_ref = bf16[1024,2048]{1,0:T(8,128)(2,1)} custom-call(s32[9]{0:T(128)S(1)} %pad_add_fusion.2.info_ref, bf16[512,1024]{1,0:T(8,128)(2,1)S(1)} %bitcast.339, bf16[512,1024]{1,0:T(8,128)(2,1)S(1)} %collective-permute-done.4.dy_mate, bf16[4096,1024]{1,0:T(8,128)(2,1)} %down_ref.3), custom_call_target="tpu_custom_call" | custom-call | flops 4294967296 | bytes 12582912 | tf_op jit(solution)/shard_map/pre/pallas_call | solution.py:445
  40.1 5.9 %qkv.3 = (bf16[8,128,1024]{2,1,0:T(8,128)(2,1)}, bf16[8,128,768]{2,1,0:T(8,128)(2,1)S(1)}) custom-call(bf16[8,64,1024]{2,1,0:T(8,128)(2,1)S(1)} %collective-permute-done.5.refs_0_, bf16[8,64,1024]{2,1,0:T(8,128)(2,1)S(1)} %collective-permute-done.6.refs_1_, f32[8,128,256]{2,1,0:T(8,128)S(1)} %pad_maximum_fusion.4.refs_2_.refs_3_, ...), custom_call_target="tpu_custom_call" | custom-call | flops 1610612736 | bytes 8388608 | tf_op jit(solution)/shard_map/qkv/pallas_call | solution.py:124
  46.0 12.5 %attend.1 = (bf16[8,64,256]{2,1,0:T(8,128)(2,1)S(1)}, bf16[8,64,256]{2,1,0:T(8,128)(2,1)S(1)}, bf16[8,64,256]{2,1,0:T(8,128)(2,1)S(1)}, bf16[8,64,256]{2,1,0:T(8...) custom-call(s32[9]{0:T(128)S(1)} %pad_add_fusion.2.info_ref, ...), custom_call_target="tpu_custom_call" | custom-call | flops 2147483648 | bytes 7340032 | tf_op jit(solution)/shard_map/attend/pallas_call | solution.py:243
  60.4 7.4 %collective-permute-done.8.refs_2_ = bf16[8,64,256]{2,1,0:T(8,128)(2,1)S(1)} collective-permute-done((bf16[8,64,256]{2,1,0:T(8,128)(2,1)S(1)}, bf16[8,64,256]{2,1,0:T(8,128)(2,1)S(1)}, u32[]{:S(2)}, u32[]{:S(2)}) %collective-permute-start.8) | collective-permute-done | bytes 262176 | tf_op jit(solution)/shard_map/ppermute | solution.py:836
  67.8 4.5 %collective-permute-done.9.refs_3_ = bf16[8,64,256]{2,1,0:T(8,128)(2,1)S(1)} collective-permute-done((bf16[8,64,256]{2,1,0:T(8,128)(2,1)S(1)}, bf16[8,64,256]{2,1,0:T(8,128)(2,1)S(1)}, u32[]{:S(2)}, u32[]{:S(2)}) %collective-permute-start.9) | collective-permute-done | bytes 262176 | tf_op jit(solution)/shard_map/ppermute | solution.py:836
  72.3 3.7 project.1
  80.1 36.2 %ffn.1 = (bf16[1024,2048]{1,0:T(8,128)(2,1)}, bf16[1024,2048]{1,0:T(8,128)(2,1)}, f32[512,1024]{1,0:T(8,128)}, bf16[512,1024]{1,0:T(8,128)(2,1)}, bf16[8,2048,128]{2,1,0:T(8,128)(2,1)}) custom-call(s32[9]{0:T(128)S(1)} %pad_add_fusion.2.info_ref, bf16[512,1024]{1,0:T(8,128)(2,1)S(1)} %get-tuple-element.137.h_own, ...), custom_call_target="tpu_custom_call" | custom-call | flops 12884901888 | bytes 16777216 | tf_op jit(solution)/shard_map/ffn/pallas_call | solution.py:517
  125.9 6.6 %mid.1 = (f32[512,1024]{1,0:T(8,128)}, bf16[512,1024]{1,0:T(8,128)(2,1)S(1)}, f32[2,1024]{1,0:T(2,128)S(1)}, bf16[8,64,256]{2,1,0:T(8,128)(2,1)S(1)}, bf16[8,64,...) custom-call(s32[9]{0:T(128)S(1)} %pad_add_fusion.2.info_ref, ...), custom_call_target="tpu_custom_call" | custom-call | flops 1073741824 | bytes 12582912 | tf_op jit(solution)/shard_map/mid/pallas_call | solution.py:627
  132.5 16.9 %ffn_rest.1 = (bf16[16,1024,128]{2,1,0:T(8,128)(2,1)}, f32[512,1024]{1,0:T(8,128)S(1)}, bf16[512,1024]{1,0:T(8,128)(2,1)}) custom-call(s32[9]{0:T(128)S(1)} %pad_add_fusion.2.info_ref, bf16[512,1024]{1,0:T(8,128)(2,1)S(1)} %copy-done.17, bf16[512,1024]{1,0:T(8,128)(2,1)S(1)} %copy-done.19, f32[512,1024]{1,0:T(8,128)} %copy-done.2, ...), custom_call_target="tpu_custom_call" | custom-call | flops 8589934592 | bytes 25165824 | tf_op jit(solution)/shard_map/ffn_rest/pallas_call | solution.py:578
  159.6 3.8 collective-permute-done.16.refs_7_
  181.8 29.4 %attend_back.1 = (bf16[8,128,768]{2,1,0:T(8,128)(2,1)S(1)}, bf16[8,128,768]{2,1,0:T(8,128)(2,1)}) custom-call(s32[9]{0:T(128)S(1)} %pad_add_fusion.2.info_ref, bf16[8,128,768]{2,1,0:T(8,128)(2,1)} %copy-done.22, bf16[8,128,768]{2,1,0:T(8,128)(2,1)} %copy-done.23, f32[8,128,256]{2,1,0:T(8,128)S(1)} %copy-done.12, f32[8,128,256]{2,1,0:T(8,128)S(1)} %copy-done.14, ...), custom_call_target="tpu_custom_call" | custom-call | flops 5368709120 | bytes 10485760 | tf_op jit(solution)/shard_map/attend_back/pallas_call | solution.py:349
  222.7 11.7 %dqkv.1 = (bf16[8,128,1024]{2,1,0:T(8,128)(2,1)}, bf16[8,128,1024]{2,1,0:T(8,128)(2,1)}, bf16[6,1024,128]{2,1,0:T(8,128)(2,1)S(1)}) custom-call(bf16[8,128,1024]{2,1,0:T(8,128)(2,1)} %get-tuple-element.178.refs_0_, bf16[8,128,1024]{2,1,0:T(8,128)(2,1)} %get-tuple-element.179.refs_1_, bf16[8,128,768]{2,1,0:T(8,128)(2,1)S(1)} %get-tuple-element.180.refs_2_, ...), custom_call_target="tpu_custom_call" | custom-call | flops 6442450944 | bytes 8388608 | tf_op jit(solution)/shard_map/dqkv/pallas_call | solution.py:712
  248.8 12.3 %collective-permute-done.30 = bf16[8,2,2,32,128]{4,3,2,1,0:T(8,128)(2,1)S(1)} collective-permute-done((bf16[8,2,2,32,128]{4,3,2,1,0:T(8,128)(2,1)S(1)}, bf16[8,2,2,32,128]{4,3,2,1,0:T(8,128)(2,1)S(1)}, u32[]{:S(2)}, u32[]{:S(2)}) %collective-permute-start.30) | collective-permute-done | bytes 262176 | tf_op jit(solution)/shard_map/ppermute | solution.py:836
  271.5 9.9 %collective-permute-done.32 = bf16[3,2,2,2,32,128]{5,4,3,2,1,0:T(8,128)(2,1)S(1)} collective-permute-done((bf16[3,2,2,2,32,128]{5,4,3,2,1,0:T(8,128)(2,1)S(1)}, bf16[3,2,2,2,32,128]{5,4,3,2,1,0:T(8,128)(2,1)S(1)}, u32[]{:S(2)}, u32[]{:S(2)}) %collective-permute-start.32) | collective-permute-done | bytes 196640 | tf_op jit(solution)/shard_map/ppermute | solution.py:836
  281.4 7.5 %collective-permute-done.33 = bf16[1792,128]{1,0:T(8,128)(2,1)S(1)} collective-permute-done((bf16[1792,128]{1,0:T(8,128)(2,1)S(1)}, bf16[1792,128]{1,0:T(8,128)(2,1)S(1)}, u32[]{:S(2)}, u32[]{:S(2)}) %collective-permute-start.33) | collective-permute-done | bytes 458784 | tf_op jit(solution)/shard_map/ppermute | solution.py:836
  299.5 10.3 %collective-permute-done.36 = bf16[1408,128]{1,0:T(8,128)(2,1)S(1)} collective-permute-done((bf16[1408,128]{1,0:T(8,128)(2,1)S(1)}, bf16[1408,128]{1,0:T(8,128)(2,1)S(1)}, u32[]{:S(2)}, u32[]{:S(2)}) %collective-permute-start.36) | collective-permute-done | bytes 360480 | tf_op jit(solution)/shard_map/ppermute | solution.py:836
  328.2 5.1 %all-to-all-done = bf16[6,4,32,128]{3,2,0,1:T(8,128)(2,1)S(1)} async-done(((bf16[6,4,32,128]{3,2,0,1:T(8,128)(2,1)}), bf16[6,4,32,128]{3,2,0,1:T(8,128)(2,1)S(1)}, u32[]{:S(2)}, u32[]{:S(2)}) %all-to-all-start) | async-done | bytes 196640 | tf_op jit(solution)/shard_map/all_to_all | solution.py:791
  343.3 4.1 all-to-all-start.2
  366.2 8.7 %collective-permute-done.48 = bf16[1280,128]{1,0:T(8,128)(2,1)} collective-permute-done((bf16[1280,128]{1,0:T(8,128)(2,1)}, bf16[1280,128]{1,0:T(8,128)(2,1)}, u32[]{:S(2)}, u32[]{:S(2)}) %collective-permute-start.48) | collective-permute-done | bytes 327712 | tf_op jit(solution)/shard_map/ppermute | solution.py:836
  374.9 9.9 %collective-permute-done.49 = bf16[1792,128]{1,0:T(8,128)(2,1)S(1)} collective-permute-done((bf16[1792,128]{1,0:T(8,128)(2,1)}, bf16[1792,128]{1,0:T(8,128)(2,1)S(1)}, u32[]{:S(2)}, u32[]{:S(2)}) %collective-permute-start.49) | collective-permute-done | bytes 458784 | tf_op jit(solution)/shard_map/ppermute | solution.py:836
  389.4 11.6 %collective-permute-done.51 = bf16[2560,128]{1,0:T(8,128)(2,1)S(1)} collective-permute-done((bf16[2560,128]{1,0:T(8,128)(2,1)S(1)}, bf16[2560,128]{1,0:T(8,128)(2,1)S(1)}, u32[]{:S(2)}, u32[]{:S(2)}) %collective-permute-start.51) | collective-permute-done | bytes 655392 | tf_op jit(solution)/shard_map/ppermute | solution.py:836
  401.0 5.3 %collective-permute-done.52 = bf16[3584,128]{1,0:T(8,128)(2,1)S(1)} collective-permute-done((bf16[3584,128]{1,0:T(8,128)(2,1)S(1)}, bf16[3584,128]{1,0:T(8,128)(2,1)S(1)}, u32[]{:S(2)}, u32[]{:S(2)}) %collective-permute-start.52) | collective-permute-done | bytes 917536 | tf_op jit(solution)/shard_map/ppermute | solution.py:836
  (443 shorter events, 168.2 us)
Async XLA Ops:
  12.0 25.4 %collective-permute-start.5 = (bf16[8,64,1024]{2,1,0:T(8,128)(2,1)S(1)}, bf16[8,64,1024]{2,1,0:T(8,128)(2,1)S(1)}, u32[]{:S(2)}, u32[]{:S(2)}) collective-permute-start(bf16[8,64,1024]{2,1,0:T(8,128)(2,1)S(1)} %bitcast.325), channel_id=1, source_target_pairs={{0,2},{1,3},{2,0},{3,1},{4,6},{5,7},{6,4},{7,5},{8,10},{9,11},{10,... | collective-permute-start | bytes 3145736 | tf_op jit(solution)/shard_map/ppermute | solution.py:836
  120.4 30.2 %collective-permute-start.12 = (bf16[4,2,2,2,128,128]{5,4,2,0,1,3:T(8,128)(2,1)S(1)}, bf16[4,2,2,2,128,128]{5,4,2,0,1,3:T(8,128)(2,1)}, u32[]{:S(2)}, u32[]{:S(2)}) collective-permute-start(bf16[4,2,2,2,128,128]{5,4,2,0,1,3:T(8,128)(2,1)S(1)} %bitcast.435), channel_id=1, source_target_pairs={{0,8},{1,9},{2,10},{3,11},{4,12},{5,13},{6,14},{7,15},{8,0},{9,1},... | collective-permute-start | bytes 3145736 | tf_op jit(solution)/shard_map/ppermute | solution.py:836
  124.3 33.1 %collective-permute-start.11 = (bf16[4,2,2,2,128,128]{5,4,1,0,3,2:T(8,128)(2,1)}, bf16[4,2,2,2,128,128]{5,4,1,0,3,2:T(8,128)(2,1)}, u32[]{:S(2)}, u32[]{:S(2)}) collective-permute-start(bf16[4,2,2,2,128,128]{5,4,1,0,3,2:T(8,128)(2,1)} %bitcast.322), channel_id=1, source_target_pairs={{0,4},{1,5},{2,6},{3,7},{4,0},{5,1},{6,2},{7,3},{8,12},{9,13},{10,... | collective-permute-start | bytes 3145736 | tf_op jit(solution)/shard_map/ppermute | solution.py:836
  165.0 46.3 %collective-permute-start.20 = (bf16[8,2,2,2,2,32,128]{6,5,4,3,2,1,0:T(8,128)(2,1)}, bf16[8,2,2,2,2,32,128]{6,5,4,3,2,1,0:T(8,128)(2,1)}, u32[]{:S(2)}, u32[]{:S(2)}) collective-permute-start(bf16[8,2,2,2,2,32,128]{6,5,4,3,2,1,0:T(8,128)(2,1)} %dynamic-slice_bitcast_fusion.1), channel_id=1, source_target_pairs={{0,2},{1,3},{2,0},{3,1},{4,6},{5,7},{6,4},{7,5},{8,10},{9,11},{10,... | collective-permute-start | bytes 3145736 | tf_op jit(solution)/shard_map/ppermute | solution.py:836
  166.6 44.7 %collective-permute-start.21 = (bf16[8,2,2,2,2,32,128]{6,5,4,3,2,1,0:T(8,128)(2,1)}, bf16[8,2,2,2,2,32,128]{6,5,4,3,2,1,0:T(8,128)(2,1)}, u32[]{:S(2)}, u32[]{:S(2)}) collective-permute-start(bf16[8,2,2,2,2,32,128]{6,5,4,3,2,1,0:T(8,128)(2,1)} %dynamic-slice_bitcast_fusion), channel_id=1, source_target_pairs={{0,4},{1,5},{2,6},{3,7},{4,0},{5,1},{6,2},{7,3},{8,12},{9,13},{10,... | collective-permute-start | bytes 3145736 | tf_op jit(solution)/shard_map/ppermute | solution.py:836
  169.7 41.6 %collective-permute-start.22 = (bf16[8,2,2,2,2,32,128]{6,5,4,3,2,0,1:T(8,128)(2,1)}, bf16[8,2,2,2,2,32,128]{6,5,4,3,2,0,1:T(8,128)(2,1)}, u32[]{:S(2)}, u32[]{:S(2)}) collective-permute-start(bf16[8,2,2,2,2,32,128]{6,5,4,3,2,0,1:T(8,128)(2,1)} %bitcast.320), channel_id=1, source_target_pairs={{0,1},{1,0},{2,3},{3,2},{4,5},{5,4},{6,7},{7,6},{8,9},{9,8},{10,11... | collective-permute-start | bytes 3145736 | tf_op jit(solution)/shard_map/ppermute | solution.py:836
  172.9 38.4 %collective-permute-start.19 = (bf16[4,2,2,128,128]{4,3,2,0,1:T(8,128)(2,1)}, bf16[4,2,2,128,128]{4,3,2,0,1:T(8,128)(2,1)}, u32[]{:S(2)}, u32[]{:S(2)}) collective-permute-start(bf16[4,2,2,128,128]{4,3,2,0,1:T(8,128)(2,1)} %dynamic-slice_bitcast_fusion.4), channel_id=1, source_target_pairs={{0,16},{1,17},{2,18},{3,19},{4,20},{5,21},{6,22},{7,23},{8,24},{9,... | collective-permute-start | bytes 1572872 | tf_op jit(solution)/shard_map/ppermute | solution.py:836
  178.9 32.4 %collective-permute-start.18 = (bf16[4,2,2,128,128]{4,3,1,0,2:T(8,128)(2,1)}, bf16[4,2,2,128,128]{4,3,1,0,2:T(8,128)(2,1)}, u32[]{:S(2)}, u32[]{:S(2)}) collective-permute-start(bf16[4,2,2,128,128]{4,3,1,0,2:T(8,128)(2,1)} %dynamic-slice_bitcast_fusion.5), channel_id=1, source_target_pairs={{0,8},{1,9},{2,10},{3,11},{4,12},{5,13},{6,14},{7,15},{8,0},{9,1},... | collective-permute-start | bytes 1572872 | tf_op jit(solution)/shard_map/ppermute | solution.py:836
  213.3 23.1 %collective-permute-start.26 = (bf16[8,2,2,2,32,128]{5,4,3,2,1,0:T(8,128)(2,1)S(1)}, bf16[8,2,2,2,32,128]{5,4,3,2,1,0:T(8,128)(2,1)S(1)}, u32[]{:S(2)}, u32[]{:S(2)}) collective-permute-start(bf16[8,2,2,2,32,128]{5,4,3,2,1,0:T(8,128)(2,1)S(1)} %dynamic-slice_bitcast_fusion.2), channel_id=1, source_target_pairs={{0,8},{1,9},{2,10},{3,11},{4,12},{5,13},{6,14},{7,15},{8,0},{9,1},... | collective-permute-start | bytes 1572872 | tf_op jit(solution)/shard_map/ppermute | solution.py:836
  216.7 19.7 %collective-permute-start.25 = (bf16[8,2,2,2,32,128]{5,4,3,2,1,0:T(8,128)(2,1)S(1)}, bf16[8,2,2,2,32,128]{5,4,3,2,1,0:T(8,128)(2,1)S(1)}, u32[]{:S(2)}, u32[]{:S(2)}) collective-permute-start(bf16[8,2,2,2,32,128]{5,4,3,2,1,0:T(8,128)(2,1)S(1)} %dynamic-slice_bitcast_fusion.3), channel_id=1, source_target_pairs={{0,4},{1,5},{2,6},{3,7},{4,0},{5,1},{6,2},{7,3},{8,12},{9,13},{10,... | collective-permute-start | bytes 1572872 | tf_op jit(solution)/shard_map/ppermute | solution.py:836
  239.2 24.0 %collective-permute-start.31 = (bf16[2,8,64,1024]{3,2,1,0:T(8,128)(2,1)S(1)}, bf16[2,8,64,1024]{3,2,1,0:T(8,128)(2,1)S(1)}, u32[]{:S(2)}, u32[]{:S(2)}) collective-permute-start(bf16[2,8,64,1024]{3,2,1,0:T(8,128)(2,1)S(1)} %pad_maximum_fusion), channel_id=1, source_target_pairs={{0,1},{1,0},{2,3},{3,2},{4,5},{5,4},{6,7},{7,6},{8,9},{9,8},{10,11... | collective-permute-start | bytes 6291464 | tf_op jit(solution)/shard_map/ppermute | solution.py:836
  240.1 21.0 %collective-permute-start.29 = (bf16[2560,128]{1,0:T(8,128)(2,1)S(1)}, bf16[2560,128]{1,0:T(8,128)(2,1)S(1)}, u32[]{:S(2)}, u32[]{:S(2)}) collective-permute-start(bf16[2560,128]{1,0:T(8,128)(2,1)S(1)} %pad_maximum_fusion.7), channel_id=1, source_target_pairs={{0,2},{1,3},{2,0},{3,1},{4,6},{5,7},{6,4},{7,5},{8,10},{9,11},{10,... | collective-permute-start | bytes 1966088 | tf_op jit(solution)/shard_map/ppermute | solution.py:836
  241.3 21.9 %collective-permute-start.28 = (bf16[2560,128]{1,0:T(8,128)(2,1)S(1)}, bf16[2560,128]{1,0:T(8,128)(2,1)S(1)}, u32[]{:S(2)}, u32[]{:S(2)}) collective-permute-start(bf16[2560,128]{1,0:T(8,128)(2,1)S(1)} %pad_maximum_fusion.6), channel_id=1, source_target_pairs={{0,8},{1,9},{2,10},{3,11},{4,12},{5,13},{6,14},{7,15},{8,0},{9,1},... | collective-permute-start | bytes 1966088 | tf_op jit(solution)/shard_map/ppermute | solution.py:836
  242.7 18.5 %collective-permute-start.27 = (bf16[2048,128]{1,0:T(8,128)(2,1)S(1)}, bf16[2048,128]{1,0:T(8,128)(2,1)S(1)}, u32[]{:S(2)}, u32[]{:S(2)}) collective-permute-start(bf16[2048,128]{1,0:T(8,128)(2,1)S(1)} %pad_maximum_fusion.9), channel_id=1, source_target_pairs={{0,4},{1,5},{2,6},{3,7},{4,0},{5,1},{6,2},{7,3},{8,12},{9,13},{10,... | collective-permute-start | bytes 1572872 | tf_op jit(solution)/shard_map/ppermute | solution.py:836
  264.3 25.2 %collective-permute-start.35 = (bf16[8,64,1024]{2,1,0:T(8,128)(2,1)S(1)}, bf16[8,64,1024]{2,1,0:T(8,128)(2,1)S(1)}, u32[]{:S(2)}, u32[]{:S(2)}) collective-permute-start(bf16[8,64,1024]{2,1,0:T(8,128)(2,1)S(1)} %slice_bitcast_fusion), channel_id=1, source_target_pairs={{0,2},{1,3},{2,0},{3,1},{4,6},{5,7},{6,4},{7,5},{8,10},{9,11},{10,... | collective-permute-start | bytes 3145736 | tf_op jit(solution)/shard_map/ppermute | solution.py:836
  267.3 21.6 %collective-permute-start.33 = (bf16[1792,128]{1,0:T(8,128)(2,1)S(1)}, bf16[1792,128]{1,0:T(8,128)(2,1)S(1)}, u32[]{:S(2)}, u32[]{:S(2)}) collective-permute-start(bf16[1792,128]{1,0:T(8,128)(2,1)S(1)} %pad_maximum_fusion.13), channel_id=1, source_target_pairs={{0,16},{1,17},{2,18},{3,19},{4,20},{5,21},{6,22},{7,23},{8,24},{9,... | collective-permute-start | bytes 1376264 | tf_op jit(solution)/shard_map/ppermute | solution.py:836
  270.7 27.8 %collective-permute-start.40 = (bf16[8,2,32,128]{3,2,1,0:T(8,128)(2,1)S(1)}, bf16[8,2,32,128]{3,2,1,0:T(8,128)(2,1)S(1)}, u32[]{:S(2)}, u32[]{:S(2)}) collective-permute-start(bf16[8,2,32,128]{3,2,1,0:T(8,128)(2,1)S(1)} %dynamic-slice_bitcast_fusion.10), channel_id=1, source_target_pairs={{0,2},{1,3},{2,0},{3,1},{4,6},{5,7},{6,4},{7,5},{8,10},{9,11},{10,... | collective-permute-start | bytes 393224 | tf_op jit(solution)/shard_map/ppermute | solution.py:836
  290.6 19.2 %collective-permute-start.38 = (bf16[1536,128]{1,0:T(8,128)(2,1)S(1)}, bf16[1536,128]{1,0:T(8,128)(2,1)S(1)}, u32[]{:S(2)}, u32[]{:S(2)}) collective-permute-start(bf16[1536,128]{1,0:T(8,128)(2,1)S(1)} %pad_maximum_fusion.16), channel_id=1, source_target_pairs={{0,8},{1,9},{2,10},{3,11},{4,12},{5,13},{6,14},{7,15},{8,0},{9,1},... | collective-permute-start | bytes 1179656 | tf_op jit(solution)/shard_map/ppermute | solution.py:836
  312.0 21.3 %collective-permute-start.43 = (bf16[768,128]{1,0:T(8,128)(2,1)}, bf16[768,128]{1,0:T(8,128)(2,1)}, u32[]{:S(2)}, u32[]{:S(2)}) collective-permute-start(bf16[768,128]{1,0:T(8,128)(2,1)} %pad_maximum_fusion.21), channel_id=1, source_target_pairs={{0,16},{1,17},{2,18},{3,19},{4,20},{5,21},{6,22},{7,23},{8,24},{9,... | collective-permute-start | bytes 589832 | tf_op jit(solution)/shard_map/ppermute | solution.py:836
  312.9 20.4 %collective-permute-start.42 = (bf16[4,2,2,128,128]{4,3,0,1,2:T(8,128)(2,1)}, bf16[4,2,2,128,128]{4,3,0,1,2:T(8,128)(2,1)S(1)}, u32[]{:S(2)}, u32[]{:S(2)}) collective-permute-start(bf16[4,2,2,128,128]{4,3,0,1,2:T(8,128)(2,1)} %maximum_select_fusion.7), channel_id=1, source_target_pairs={{0,8},{1,9},{2,10},{3,11},{4,12},{5,13},{6,14},{7,15},{8,0},{9,1},... | collective-permute-start | bytes 1572872 | tf_op jit(solution)/shard_map/ppermute | solution.py:836
  336.1 17.9 %collective-permute-start.47 = (bf16[16,2,32,128]{3,2,1,0:T(8,128)(2,1)}, bf16[16,2,32,128]{3,2,1,0:T(8,128)(2,1)S(1)}, u32[]{:S(2)}, u32[]{:S(2)}) collective-permute-start(bf16[16,2,32,128]{3,2,1,0:T(8,128)(2,1)} %maximum_select_fusion.22), channel_id=1, source_target_pairs={{0,8},{1,9},{2,10},{3,11},{4,12},{5,13},{6,14},{7,15},{8,0},{9,1},... | collective-permute-start | bytes 786440 | tf_op jit(solution)/shard_map/ppermute | solution.py:836
  359.4 25.4 %collective-permute-start.50 = (bf16[16,2,2,32,128]{4,3,2,1,0:T(8,128)(2,1)}, bf16[16,2,2,32,128]{4,3,2,1,0:T(8,128)(2,1)}, u32[]{:S(2)}, u32[]{:S(2)}) collective-permute-start(bf16[16,2,2,32,128]{4,3,2,1,0:T(8,128)(2,1)} %maximum_select_fusion.8), channel_id=1, source_target_pairs={{0,4},{1,5},{2,6},{3,7},{4,0},{5,1},{6,2},{7,3},{8,12},{9,13},{10,... | collective-permute-start | bytes 1572872 | tf_op jit(solution)/shard_map/ppermute | solution.py:836
  363.7 21.2 %collective-permute-start.49 = (bf16[1792,128]{1,0:T(8,128)(2,1)}, bf16[1792,128]{1,0:T(8,128)(2,1)S(1)}, u32[]{:S(2)}, u32[]{:S(2)}) collective-permute-start(bf16[1792,128]{1,0:T(8,128)(2,1)} %pad_maximum_fusion.14), channel_id=1, source_target_pairs={{0,16},{1,17},{2,18},{3,19},{4,20},{5,21},{6,22},{7,23},{8,24},{9,... | collective-permute-start | bytes 1376264 | tf_op jit(solution)/shard_map/ppermute | solution.py:836
  386.9 19.4 %collective-permute-start.52 = (bf16[3584,128]{1,0:T(8,128)(2,1)S(1)}, bf16[3584,128]{1,0:T(8,128)(2,1)S(1)}, u32[]{:S(2)}, u32[]{:S(2)}) collective-permute-start(bf16[3584,128]{1,0:T(8,128)(2,1)S(1)} %pad_maximum_fusion.5), channel_id=1, source_target_pairs={{0,8},{1,9},{2,10},{3,11},{4,12},{5,13},{6,14},{7,15},{8,0},{9,1},... | collective-permute-start | bytes 2752520 | tf_op jit(solution)/shard_map/ppermute | solution.py:836
  (106 other events, 857.1 us)
where the time goes:
time: 421 us; the launch traced here: 414 us
  Pallas kernels  153 us (36%)
  waiting for transfers between devices  115 us (27%)
  starting transfers between devices  60 us (14%)
  other arithmetic  44.4 us (11%)
  local copies, waits for them, and re-layouts  39.3 us (9%)
    ppermute x53, waiting for transfers between devices, swap(): return lax.ppermute(a, AXES, [(i, i ^ step) for i in range(n)])  106 us
    ppermute x53, starting transfers between devices, swap(): return lax.ppermute(a, AXES, [(i, i ^ step) for i in range(n)])  49.3 us
    pallas_call x1, Pallas kernels, ffn_call(): pl.pallas_call(ffn_kernel, grid_spec=grid_spec, out_shape=[jax.ShapeDtype...  36.2 us
    pallas_call x1, Pallas kernels, attend_back_call(): pl.pallas_call(functools.partial(attend_back_kernel, groups, local, patch...  29.4 us
    pallas_call x1, Pallas kernels, ffn_rest_call(): pl.pallas_call(ffn_rest_kernel, grid_spec=grid_spec, out_shape=[jax.Shape...  16.9 us
    convert_element_type x36, other arithmetic, hops(): a = (keep.astype(F32) + got.astype(F32)).astype(BF)  14.7 us
    unnamed x136, local copies, waits for them, and re-layouts  13.4 us
    pallas_call x1, Pallas kernels, attend_call(): pl.pallas_call(functools.partial(attend_kernel, groups, local, patches, f...  12.5 us
  transfers between devices with their start and end apart: 56, of which 22 were waited for; matrix products, arithmetic and copies ran while one was open for 12% of the time, Pallas kernels for 21%

commit v1 on v0

v1 whole, which is shorter than its diff:
```python
import functools
import math

import jax
import jax.numpy as jnp
from jax import lax
from jax.experimental import pallas as pl
from jax.experimental.pallas import tpu as pltpu
from jax.sharding import PartitionSpec as P

GRID = 16
EPS = 1e-06
THETA = 10000.0
MASKED = -1e30
LIMIT = 40 * 1024 * 1024
BF = jnp.bfloat16
F32 = jnp.float32
AXES = ("batch", "patch")


def nn(a, b):
    return lax.dot_general(a, b, (((1,), (0,)), ((), ())), preferred_element_type=F32)


def nt(a, b):
    return lax.dot_general(a, b, (((1,), (1,)), ((), ())), preferred_element_type=F32)


def tn(a, b):
    return lax.dot_general(a, b, (((0,), (0,)), ((), ())), preferred_element_type=F32)


def params(*semantics):
    return pltpu.CompilerParams(
        dimension_semantics=semantics, vmem_limit_bytes=LIMIT
    )


def cost(micros):
    return pl.CostEstimate(flops=int(micros * 2.875e+08), bytes_accessed=1, transcendentals=0)


def full(shape, memory=None):
    zeros = (0,) * len(shape)
    return pl.BlockSpec(shape, lambda *_: zeros)


def blocked(ref, value):
    for n in range(ref.shape[0]):
        ref[n] = value[:, n * 128 : (n + 1) * 128].astype(BF)


def hbm(a):
    return pltpu.with_memory_space_constraint(a, pltpu.HBM)


def smem():
    return pl.BlockSpec(memory_space=pltpu.SMEM)


def normalise(x):
    mean = jnp.mean(x, axis=-1, keepdims=True)
    centred = x - mean
    spread = jnp.mean(centred * centred, axis=-1, keepdims=True)
    rstd = lax.rsqrt(spread + EPS)
    return centred * rstd, rstd


def norm_back(d_h, hat, rstd, gain):
    d_hat = d_h * gain
    first = jnp.mean(d_hat, axis=-1, keepdims=True)
    second = jnp.mean(d_hat * hat, axis=-1, keepdims=True)
    return rstd * (d_hat - first - hat * second)


def partner(value):
    head = 64
    half = head // 6
    width = value.shape[1]
    ahead = jnp.concatenate([value[:, half:], value[:, :half]], axis=1)
    behind = jnp.concatenate([value[:, width - half :], value[:, : width - half]], axis=1)
    lane = lax.broadcasted_iota(jnp.int32, value.shape, 1) % head
    return jnp.where(lane % (2 * half) < half, ahead, behind)


def qkv_kernel(count, local, *refs):
    tok = refs[:count]
    cs_ref, w_ref, gain_ref, shift_ref = refs[count : count + 4]
    h_ref, qkv_ref = refs[count + 4 :]
    x = jnp.concatenate([t[...] for t in tok], axis=1)
    fb, rows, dim = x.shape
    x = x.reshape(fb * rows, dim).astype(F32)
    hat, _ = normalise(x)
    h = (hat * gain_ref[...] + shift_ref[...]).astype(BF)
    h_ref[...] = h.reshape(fb, rows, dim)
    y = nn(h, w_ref[...])
    cs = cs_ref[...].reshape(fb * rows, 256)
    cos = cs[:, :128]
    sin = cs[:, 128:]
    for at in range(0, 3 * local, 384):
        q = y[:, at : at + 128]
        k = y[:, at + 128 : at + 256]
        q = (q * cos + partner(q) * sin).astype(BF) * BF(0.125)
        k = (k * cos + partner(k) * sin).astype(BF)
        v = y[:, at + 256 : at + 384].astype(BF)
        qkv_ref[:, :, at : at + 128] = q.reshape(fb, rows, 128)
        qkv_ref[:, :, at + 128 : at + 256] = k.reshape(fb, rows, 128)
        qkv_ref[:, :, at + 256 : at + 384] = v.reshape(fb, rows, 128)


def qkv_call(items, cs, w_local, gain, shift):
    count = len(items)
    frames, width, dim = items[0].shape
    local = w_local.shape[1] // 3
    rows = count * width
    fb = max(1, min(frames, 512 // rows))
    while frames % fb:
        fb -= 1
    shapes = [
        pltpu.HBM((frames, rows, dim), BF),
        pltpu.HBM((frames, rows, 3 * local), BF),
    ]
    return pl.pallas_call(
        functools.partial(qkv_kernel, count, local),
        grid=(frames // fb,),
        in_specs=[pl.BlockSpec((fb, width, dim), lambda i: (i, 0, 0))] * count
        + [
            pl.BlockSpec((fb, rows, 256), lambda i: (i, 0, 0)),
            full(w_local.shape),
            full(gain.shape),
            full(shift.shape),
        ],
        out_specs=[
            pl.BlockSpec((fb, rows, dim), lambda i: (i, 0, 0)),
            pl.BlockSpec((fb, rows, 3 * local), lambda i: (i, 0, 0)),
        ],
        out_shape=shapes,
        compiler_params=params("arbitrary"),
        cost_estimate=cost(5.5),
        name="qkv",
    )(*items, cs, w_local, gain, shift)


def lane_halves(shape):
    lane = lax.broadcasted_iota(jnp.int32, shape, 1)
    return lane < 64


def attend_kernel(groups, local, patches, most, info_ref, *refs):
    ins = refs[:groups]
    o_refs = refs[groups : groups + patches]
    of_ref, lse_ref = refs[groups + patches :]
    f = pl.program_id(0)
    begin = info_ref[1 + f]
    rows = sum(r.shape[1] for r in ins)
    low = lane_halves((rows, 128))
    one = jnp.ones((rows, 128), BF)
    zero = jnp.zeros((rows, 128), BF)
    lane = lax.broadcasted_iota(jnp.int32, (rows, 128), 1)

    def part_of(g, pair, n):
        at = pair * 384 + n * 128
        return jnp.concatenate([r[g, :, at : at + 128] for r in ins], axis=0)

    def finish(pair, tops, accs, lses):
        num = jnp.where(low, accs[0], accs[1])
        den = pltpu.roll(jnp.where(low, accs[1], accs[0]), 64, 1)
        of_ref[0, :, pair * 128 : (pair + 1) * 128] = num / den
        logs = jnp.log(jnp.where(low, accs[1], accs[0]))
        lses = jnp.where(lane == 2 * pair + 64, tops[0] + logs, lses)
        return jnp.where(lane == 2 * pair + 1, tops[1] + logs, lses)

    def store(lses):
        even = lane % 2 == 0
        lses = jnp.where(even, pltpu.roll(lses, 64, 1), lses)
        lse_ref[0] = lses.T[:8]

    def whole(count):
        lses = jnp.zeros((rows, 128), F32)
        for pair in range(local // 128):
            q = part_of(f, pair, 0)
            tops, accs = [], []
            for h in range(2):
                qm = jnp.where(low == (h == 0), q, zero)
                scores = [nt(qm, part_of(begin + n, pair, 1)) for n in range(count)]
                top = scores[0]
                for s in scores[1:]:
                    top = jnp.maximum(top, s)
                top = jnp.max(top, axis=1, keepdims=True)
                acc = None
                for n, s in enumerate(scores):
                    v = jnp.where(low == (h == 0), part_of(begin + n, pair, 2), one)
                    part = nn(jnp.exp(s - top).astype(BF), v)
                    acc = part if acc is None else acc + part
                tops.append(top)
                accs.append(acc)
            lses = finish(pair, tops, accs, lses)
        store(lses)

    if most <= 4:
        for count in range(1, most + 1):
            pl.when(f + 1 - begin == count)(functools.partial(whole, count))
    else:
        lses = jnp.zeros((rows, 128), F32)
        for pair in range(local // 128):
            q = part_of(f, pair, 0)

            def body(g, state, pair=pair, q=q):
                new = []
                for h in range(2):
                    top, acc = state[2 * h : 2 * h + 2]
                    qm = jnp.where(low == (h == 0), q, zero)
                    s = nt(qm, part_of(g, pair, 1))
                    new_top = jnp.maximum(top, jnp.max(s, axis=1, keepdims=True))
                    v = jnp.where(low == (h == 0), part_of(g, pair, 2), one)
                    p = jnp.exp(s - new_top).astype(BF)
                    new += [new_top, acc * jnp.exp(top - new_top) + nn(p, v)]
                return tuple(new)

            blank = (jnp.full((rows, 1), MASKED, F32), jnp.zeros((rows, 128), F32))
            state = lax.fori_loop(begin, f + 1, body, blank + blank)
            lses = finish(pair, state[0::2], state[1::2], lses)
        store(lses)

    o = of_ref[0].astype(BF)
    width = rows // patches
    for j in range(patches):
        o_refs[j][0] = o[j * width : (j + 1) * width]


def attend_call(info, qkv, patches):
    groups = len(qkv)
    frames = qkv[0].shape[0]
    local = qkv[0].shape[2] // 3
    rows = sum(a.shape[1] for a in qkv)
    width = rows // patches
    shapes = [jax.ShapeDtypeStruct((frames, width, local), BF)] * patches
    sizes = [(frames, width, local)] * patches + [(frames, rows, local), (frames, 8, rows)]
    shapes += [pltpu.HBM((frames, rows, local), F32), pltpu.HBM((frames, 8, rows), F32)]
    return pl.pallas_call(
        functools.partial(attend_kernel, groups, local, patches, frames // 2),
        grid=(frames,),
        in_specs=[smem()] + [full(a.shape) for a in qkv],
        out_specs=[pl.BlockSpec((1,) + s[1:], lambda i: (i, 0, 0)) for s in sizes],
        out_shape=shapes,
        compiler_params=params("arbitrary"),
        cost_estimate=cost(12.5),
        name="attend",
    )(info, *[hbm(a) for a in qkv])


def attend_back_kernel(groups, pair, patches, info_ref, *refs):
    ins = refs[:groups]
    css = refs[groups : 2 * groups]
    do_refs = refs[2 * groups : 2 * groups + patches]
    refs = refs[2 * groups + patches :]
    of_ref, lse_ref = refs[:2]
    outs = refs[2 : groups + 2]
    dk_ref, dv_ref, dq_ref, kt_ref = refs[groups + 2 :]
    f = pl.program_id(0)
    frames = pl.num_programs(0)
    begin = info_ref[1 + f]

    def part_of(g, n):
        return jnp.concatenate([r[g, :, n * 128 : (n + 1) * 128] for r in ins], axis=0)

    q = part_of(f, 0)
    d_o = jnp.concatenate([r[0] for r in do_refs], axis=0)
    rows = q.shape[0]
    low = lane_halves((rows, 128))
    zero = jnp.zeros((rows, 128), BF)
    turned = (d_o.astype(F32) * of_ref[0]).T
    delta = [jnp.sum(turned[h * 64 : (h + 1) * 64], axis=0, keepdims=True) for h in range(2)]
    lse = lse_ref[0, 2 * pair : 2 * pair + 2]
    dk_ref[f] = jnp.zeros((rows, 128), F32)
    dv_ref[f] = jnp.zeros((rows, 128), F32)
    dq_ref[...] = jnp.zeros((128, rows), F32)
    kt_ref[f] = part_of(f, 1).T
    qm = [jnp.where(low == (h == 0), q, zero) for h in range(2)]
    dom = [jnp.where(low == (h == 0), d_o, zero) for h in range(2)]

    @pl.loop(begin, f + 1)
    def _(g):
        k = part_of(g, 1)
        v = part_of(g, 2)
        scores = [nt(k, qm[h]) for h in range(2)]
        dps = [nt(v, dom[h]) for h in range(2)]
        dk = dv = None
        for h in range(2):
            p = jnp.exp(scores[h] - lse[h : h + 1])
            ds = (p * (dps[h] - delta[h])).astype(BF)
            dq_ref[h * 64 : (h + 1) * 64] += nn(kt_ref[g, h * 64 : (h + 1) * 64], ds)
            part_k = nn(ds, qm[h])
            part_v = nn(p.astype(BF), dom[h])
            dk = part_k if dk is None else dk + part_k
            dv = part_v if dv is None else dv + part_v
        dk_ref[g] += dk
        dv_ref[g] += dv

    def turn_back(t, value):
        cs = jnp.concatenate([r[t] for r in css], axis=0)
        return (value * cs[:, :128] - partner(value) * cs[:, 128:]).astype(BF)

    def put(t, n, value):
        start = 0
        for out in outs:
            count = out.shape[1]
            out[t, :, n * 128 : (n + 1) * 128] = value[start : start + count]
            start += count

    put(f, 0, turn_back(f, dq_ref[...].T * 0.125))

    @pl.when(f == frames - 1)
    def _():
        @pl.loop(0, frames)
        def _(t):
            put(t, 1, turn_back(t, dk_ref[t]))
            put(t, 2, dv_ref[t].astype(BF))


def attend_back_call(info, qkv, cs, d_o, o_full, lse, patches, pair):
    groups = len(qkv)
    frames = qkv[0].shape[0]
    rows = sum(a.shape[1] for a in qkv)
    width = rows // patches
    shapes = [jax.ShapeDtypeStruct((frames, a.shape[1], 384), BF) for a in qkv]
    return pl.pallas_call(
        functools.partial(attend_back_kernel, groups, pair, patches),
        grid=(frames,),
        in_specs=[smem()]
        + [pl.BlockSpec(a.shape[:2] + (384,), lambda i: (0, 0, pair)) for a in qkv]
        + [full(a.shape) for a in cs]
        + [pl.BlockSpec((1, width, 128), lambda i: (i, 0, pair))] * patches
        + [
            pl.BlockSpec((1, rows, 128), lambda i: (i, 0, pair)),
            pl.BlockSpec((1, 8, rows), lambda i: (i, 0, 0)),
        ],
        out_specs=[full(s.shape) for s in shapes],
        out_shape=shapes,
        scratch_shapes=[
            pltpu.VMEM((frames, rows, 128), F32),
            pltpu.VMEM((frames, rows, 128), F32),
            pltpu.VMEM((128, rows), F32),
            pltpu.VMEM((frames, 128, rows), BF),
        ],
        compiler_params=params("arbitrary"),
        cost_estimate=cost(15),
        name="attend_back",
    )(info, *[hbm(a) for a in (*qkv, *cs)], *d_o, hbm(o_full), hbm(lse))


def heads_rows(info_ref, j, local):
    return pl.ds(pl.multiple_of((info_ref[0] ^ j) * local, local), local)


def project_kernel(patches, info_ref, *refs):
    o_refs = refs[:patches]
    x_ref, w_ref, gain_ref, shift_ref, x1_ref, h_ref, o_ref, kept_ref = refs[patches:]
    fb, width, local = o_refs[0].shape
    rows = fb * width
    for j, ref in enumerate(o_refs):
        kept_ref[j] = ref[...].reshape(rows, local)
    o = jnp.concatenate([kept_ref[info_ref[0] ^ p] for p in range(patches)], axis=1)
    o_ref[...] = o
    acc = x_ref[...].astype(F32).reshape(rows, -1) + nn(o, w_ref[...])
    x1_ref[...] = acc
    hat, _ = normalise(acc)
    h_ref[...] = (hat * gain_ref[...] + shift_ref[...]).astype(BF)


def project_call(info, o_in, tokens, w_out, gain, shift):
    patches = len(o_in)
    frames, width, local = o_in[0].shape
    dim = w_out.shape[0]
    fb = frames // 2
    rows = frames * width
    return pl.pallas_call(
        functools.partial(project_kernel, patches),
        grid=(2,),
        in_specs=[smem()]
        + [pl.BlockSpec((fb, width, local), lambda i: (i, 0, 0))] * patches
        + [
            pl.BlockSpec((fb, width, dim), lambda i: (i, 0, 0)),
            full(w_out.shape),
            full(gain.shape),
            full(shift.shape),
        ],
        out_specs=[
            pl.BlockSpec((rows // 2, dim), lambda i: (i, 0)),
            pl.BlockSpec((rows // 2, dim), lambda i: (i, 0)),
            pl.BlockSpec((rows // 2, dim), lambda i: (i, 0)),
        ],
        out_shape=[
            pltpu.HBM((rows, dim), F32),
            jax.ShapeDtypeStruct((rows, dim), BF),
            jax.ShapeDtypeStruct((rows, dim), BF),
        ],
        scratch_shapes=[pltpu.VMEM((patches, rows // 2, local), BF)],
        compiler_params=params("arbitrary"),
        cost_estimate=cost(3.7),
        name="project",
    )(info, *o_in, tokens, w_out, gain, shift)


def tile_at(piece, steps):
    return lambda i, info: ((i % steps) * 2 + (info[0] & 1)) * 2 + (
        i // steps if piece is None else piece
    )


def pre_kernel(info_ref, dy_own, dy_mate, down_ref, dg_ref):
    half = dy_own.shape[0]
    dg_ref[:half] = nt(dy_own[...], down_ref[...]).astype(BF)
    dg_ref[half:] = nt(dy_mate[...], down_ref[...]).astype(BF)


def pre_call(info, dy_own, dy_mate, w_down, patches):
    half, dim = dy_own.shape
    hidden = w_down.shape[0]
    tile, steps = hidden // patches // 2, patches // 2
    at = tile_at(None, steps)
    return pl.pallas_call(
        pre_kernel,
        grid_spec=pltpu.PrefetchScalarGridSpec(
            num_scalar_prefetch=1,
            grid=(2 * steps,),
            in_specs=[full((half, dim))] * 2
            + [pl.BlockSpec((tile, dim), lambda i, info: (at(i, info), 0))],
            out_specs=pl.BlockSpec((2 * half, tile), lambda i, info: (0, i)),
        ),
        out_shape=pltpu.HBM((2 * half, hidden // 2), BF),
        compiler_params=params("arbitrary"),
        cost_estimate=cost(8.5),
        name="pre",
    )(info, dy_own, dy_mate, w_down)


def ffn_kernel(
    info_ref, h_own, h_mate, dy_own, dy_mate, dg_ref, up_ref,
    g_ref, du_ref, dw0_ref, dw1_ref, dh_own, dh_mate, acc_ref,
):
    step = pl.program_id(0)
    half = h_own.shape[0]

    @pl.when(step == 0)
    def _():
        acc_ref[...] = jnp.zeros(acc_ref.shape, F32)

    w_up = up_ref[...]
    total = None
    chunk = half // 2
    for n in range(4):
        h_ref, dy_ref = ((h_own, dy_own), (h_mate, dy_mate))[n // 2]
        here = slice((n % 2) * chunk, (n % 2 + 1) * chunk)
        rows = slice(n * chunk, (n + 1) * chunk)
        u = nn(h_ref[here], w_up)
        cdf = 0.5 + 0.5 * lax.erf(u * math.sqrt(0.5))
        pdf = jnp.exp(u * u * -0.5) * (1.0 / math.sqrt(2.0 * math.pi))
        g = (u * cdf).astype(BF)
        du = (dg_ref[rows].astype(F32) * (cdf + u * pdf)).astype(BF)
        g_ref[rows] = g
        du_ref[rows] = du
        acc_ref[rows] += nt(du, w_up)
        dw = tn(g, dy_ref[here])
        total = dw if total is None else total + dw
    middle = total.shape[1] // 2
    blocked(dw0_ref, total[:, :middle])
    blocked(dw1_ref, total[:, middle:])

    @pl.when(step == pl.num_programs(0) - 1)
    def _():
        dh_own[...] = acc_ref[:half]
        dh_mate[...] = acc_ref[half:].astype(BF)


def ffn_call(info, h_own, h_mate, dy_own, dy_mate, dg, w_up, patches):
    half, dim = h_own.shape
    hidden = w_up.shape[1]
    tile, steps = hidden // patches // 2, patches // 2
    at = tile_at(None, steps)
    column = pl.BlockSpec((2 * half, tile), lambda i, info: (0, i))
    return pl.pallas_call(
        ffn_kernel,
        grid_spec=pltpu.PrefetchScalarGridSpec(
            num_scalar_prefetch=1,
            grid=(2 * steps,),
            in_specs=[full((half, dim))] * 4
            + [column, pl.BlockSpec((dim, tile), lambda i, info: (0, at(i, info)))],
            out_specs=[
                column,
                column,
                pl.BlockSpec((dim // 256, tile, 128), lambda i, info: (0, i, 0)),
                pl.BlockSpec((dim // 256, tile, 128), lambda i, info: (0, i, 0)),
                full((half, dim)),
                full((half, dim)),
            ],
            scratch_shapes=[pltpu.VMEM((2 * half, dim), F32)],
        ),
        out_shape=[
            pltpu.HBM((2 * half, hidden // 2), BF),
            pltpu.HBM((2 * half, hidden // 2), BF),
            pltpu.HBM((dim // 256, hidden // 2, 128), BF),
            pltpu.HBM((dim // 256, hidden // 2, 128), BF),
            pltpu.HBM((half, dim), F32),
            jax.ShapeDtypeStruct((half, dim), BF),
        ],
        compiler_params=params("arbitrary"),
        cost_estimate=cost(25),
        name="ffn",
    )(info, h_own, h_mate, hbm(dy_own), hbm(dy_mate), hbm(dg), hbm(w_up))


def up_kernel(steps, tile, h_own, h_mate, du_ref, o_own, o_mate, da_own, da_mate, dw_ref):
    half = h_own.shape[0]
    step = pl.program_id(0)
    count = tile // 128

    def put(at, value):
        for n in range(value.shape[1] // 128):
            dw_ref[at + n] = value[:, n * 128 : (n + 1) * 128].astype(BF)

    @pl.when(step < steps)
    def _():
        value = tn(h_own[...], du_ref[:half]) + tn(h_mate[...], du_ref[half:])
        put(step * count, value)

    @pl.when(step == steps)
    def _():
        put(steps * count, tn(o_own[...], da_own[...]) + tn(o_mate[...], da_mate[...]))


def up_call(info, h_own, h_mate, du, o_own, o_mate, da_own, da_mate, patches, piece):
    half, dim = h_own.shape
    columns = du.shape[1] // 2
    steps = patches // 2
    tile = columns // steps
    shape = (columns // 128 + dim // 512, dim, 128)
    quarter = pl.BlockSpec((half, dim // 4), lambda i, info: (0, (info[0] & 1) * 2 + piece))

    def kernel(info_ref, *refs):
        up_kernel(steps, tile, *refs)

    return pl.pallas_call(
        kernel,
        grid_spec=pltpu.PrefetchScalarGridSpec(
            num_scalar_prefetch=1,
            grid=(steps + 1,),
            in_specs=[full((half, dim))] * 2
            + [
                pl.BlockSpec(
                    (2 * half, tile),
                    lambda i, info: (0, piece * steps + jnp.minimum(i, steps - 1)),
                )
            ]
            + [full((half, dim))] * 2
            + [quarter] * 2,
            out_specs=full(shape),
        ),
        out_shape=jax.ShapeDtypeStruct(shape, BF),
        compiler_params=params("arbitrary"),
        cost_estimate=cost(6),
        name="up",
    )(info, hbm(h_own), hbm(h_mate), hbm(du), hbm(o_own), hbm(o_mate), hbm(da_own), hbm(da_mate))


def down_kernel(info_ref, x1_ref, g0_ref, g1_ref, down0_ref, down1_ref, own_ref, mate_ref, acc_ref):
    step = pl.program_id(0)
    half = x1_ref.shape[0]

    @pl.when(step == 0)
    def _():
        acc_ref[:half] = x1_ref[...]
        acc_ref[half:] = jnp.zeros_like(x1_ref)

    for n in range(2):
        rows = slice(n * half, (n + 1) * half)
        acc_ref[rows] += nn(g0_ref[rows], down0_ref[...]) + nn(g1_ref[rows], down1_ref[...])

    @pl.when(step == pl.num_programs(0) - 1)
    def _():
        own_ref[...] = acc_ref[:half]
        mate_ref[...] = acc_ref[half:].astype(BF)


def down_call(info, x1, g, w_down, patches):
    half, dim = x1.shape
    hidden = w_down.shape[0]
    tile, steps = hidden // patches // 2, patches // 2
    first, second = tile_at(0, steps), tile_at(1, steps)
    return pl.pallas_call(
        down_kernel,
        grid_spec=pltpu.PrefetchScalarGridSpec(
            num_scalar_prefetch=1,
            grid=(steps,),
            in_specs=[
                full((half, dim)),
                pl.BlockSpec((2 * half, tile), lambda i, info: (0, i)),
                pl.BlockSpec((2 * half, tile), lambda i, info: (0, steps + i)),
                pl.BlockSpec((tile, dim), lambda i, info: (first(i, info), 0)),
                pl.BlockSpec((tile, dim), lambda i, info: (second(i, info), 0)),
            ],
            out_specs=[full((half, dim)), full((half, dim))],
            scratch_shapes=[pltpu.VMEM((2 * half, dim), F32)],
        ),
        out_shape=[
            jax.ShapeDtypeStruct((half, dim), F32),
            jax.ShapeDtypeStruct((half, dim), BF),
        ],
        compiler_params=params("arbitrary"),
        cost_estimate=cost(8.5),
        name="down",
    )(info, hbm(x1), hbm(g), hbm(g), hbm(w_down), hbm(w_down))


def mid_kernel(
    patches, info_ref, dh_ref, recv_ref, x1_ref, dy_ref, w_ref, gain_ref, dx_ref, da_ref, gs_ref,
    *do_refs,
):
    step = pl.program_id(0)
    fb, width, local = do_refs[0].shape
    hat, rstd = normalise(x1_ref[...])
    dh = dh_ref[...] + recv_ref[...].astype(F32)
    dx = dy_ref[...].astype(F32) + norm_back(dh, hat, rstd, gain_ref[...])
    dx_ref[...] = dx
    da = dx.astype(BF)
    da_ref[...] = da
    sums = jnp.concatenate(
        [jnp.sum(dh * hat, axis=0, keepdims=True), jnp.sum(dh, axis=0, keepdims=True)], axis=0
    )

    @pl.when(step == 0)
    def _():
        gs_ref[...] = sums

    @pl.when(step > 0)
    def _():
        gs_ref[...] += sums

    for j, do_ref in enumerate(do_refs):
        part = nt(da, w_ref[heads_rows(info_ref, j, local), :])
        do_ref[...] = part.astype(BF).reshape(fb, width, local)


def mid_call(info, dh, recv, x1, dy, w_out, gain, frames, patches):
    rows, dim = x1.shape
    width = rows // frames
    local = dim // patches
    fb = frames // 2
    row = pl.BlockSpec((rows // 2, dim), lambda i: (i, 0))
    return pl.pallas_call(
        functools.partial(mid_kernel, patches),
        grid=(2,),
        in_specs=[smem(), row, row, row, row, full(w_out.shape), full(gain.shape)],
        out_specs=[row, row, full((2, dim))]
        + [pl.BlockSpec((fb, width, local), lambda i: (i, 0, 0))] * patches,
        out_shape=[
            pltpu.HBM((rows, dim), F32),
            jax.ShapeDtypeStruct((rows, dim), BF),
            jax.ShapeDtypeStruct((2, dim), F32),
        ]
        + [jax.ShapeDtypeStruct((frames, width, local), BF)] * patches,
        compiler_params=params("arbitrary"),
        cost_estimate=cost(6),
        name="mid",
    )(info, hbm(dh), recv, hbm(x1), hbm(dy), hbm(w_out), gain)


def dwq_kernel(groups, *refs):
    hs, ds = refs[:groups], refs[groups : 2 * groups]
    dw_ref, acc_ref = refs[2 * groups :]
    step = pl.program_id(0)

    @pl.when(step == 0)
    def _():
        acc_ref[...] = jnp.zeros(acc_ref.shape, F32)

    total = None
    for h_ref, d_ref in zip(hs, ds):
        fb, rows, dim = h_ref.shape
        part = tn(h_ref[...].reshape(fb * rows, dim), d_ref[...].reshape(fb * rows, -1))
        total = part if total is None else total + part
    acc_ref[...] += total

    @pl.when(step == pl.num_programs(0) - 1)
    def _():
        blocked(dw_ref, acc_ref)


def frame_blocks(a, fb):
    return pl.BlockSpec((fb,) + a.shape[1:], lambda i: (i, 0, 0))


def dwq_call(hs, ds):
    groups = len(hs)
    frames, _, dim = hs[0].shape
    fb = max(1, frames // 2 if frames <= 8 else frames // 8)
    return pl.pallas_call(
        functools.partial(dwq_kernel, groups),
        grid=(frames // fb,),
        in_specs=[frame_blocks(a, fb) for a in (*hs, *ds)],
        out_specs=full((3, dim, 128)),
        out_shape=jax.ShapeDtypeStruct((3, dim, 128), BF),
        scratch_shapes=[pltpu.VMEM((dim, 384), F32)],
        compiler_params=params("arbitrary"),
        cost_estimate=cost(4.3),
        name="dwq",
    )(*[hbm(a) for a in hs], *ds)


def dh_kernel(groups, pairs, width, *refs):
    ds = [refs[n * groups : (n + 1) * groups] for n in range(pairs)]
    w_ref, even_ref, odd_ref = refs[pairs * groups :]
    j = 0
    for n in range(groups):
        fb, rows, _ = ds[0][n].shape
        d = jnp.concatenate([ds[p][n][...] for p in range(pairs)], axis=2)
        dh = nt(d.reshape(fb * rows, -1), w_ref[...]).astype(BF).reshape(fb, rows, -1)
        for at in range(0, rows, width):
            out = odd_ref if j % 2 else even_ref
            out[j // 2] = dh[:, at : at + width]
            j += 1


def dh_call(ds, w_local, patches):
    pairs, groups = len(ds), len(ds[0])
    frames = ds[0][0].shape[0]
    rows = sum(a.shape[1] for a in ds[0])
    width = rows // patches
    dim = w_local.shape[0]
    fb = max(1, frames // 4 if frames <= 8 else frames // 16)
    shape = (patches // 2, frames, width, dim)
    block = pl.BlockSpec((patches // 2, fb, width, dim), lambda i: (0, i, 0, 0))
    return pl.pallas_call(
        functools.partial(dh_kernel, groups, pairs, width),
        grid=(frames // fb,),
        in_specs=[frame_blocks(a, fb) for d in ds for a in d] + [full(w_local.shape)],
        out_specs=[block, block],
        out_shape=[jax.ShapeDtypeStruct(shape, BF)] * 2,
        compiler_params=params("arbitrary"),
        cost_estimate=cost(5),
        name="dh",
    )(*[a for d in ds for a in d], w_local)


def last_kernel(a_ref, b_ref, x_ref, dx_ref, gain_ref, gt_ref, gs_ref):
    step = pl.program_id(0)
    hat, rstd = normalise(x_ref[...].astype(F32))
    dh = a_ref[...].astype(F32) + b_ref[...].astype(F32)
    gt_ref[...] = (dx_ref[...] + norm_back(dh, hat, rstd, gain_ref[...])).astype(BF)
    sums = jnp.concatenate(
        [jnp.sum(dh * hat, axis=0, keepdims=True), jnp.sum(dh, axis=0, keepdims=True)], axis=0
    )

    @pl.when(step == 0)
    def _():
        gs_ref[...] = sums

    @pl.when(step > 0)
    def _():
        gs_ref[...] += sums


def last_call(a, b, x, dx, gain):
    rows, dim = x.shape
    row = pl.BlockSpec((rows // 2, dim), lambda i: (i, 0))
    return pl.pallas_call(
        last_kernel,
        grid=(2,),
        in_specs=[row, row, row, row, full(gain.shape)],
        out_specs=[row, full((2, dim))],
        out_shape=[
            jax.ShapeDtypeStruct((rows, dim), BF),
            jax.ShapeDtypeStruct((2, dim), F32),
        ],
        compiler_params=params("arbitrary"),
        cost_estimate=cost(3),
        name="last",
    )(a, b, hbm(x), hbm(dx), gain)


class Chain:
    def __init__(self, hops):
        self.hops, self.value, self.got, self.begun, self.done = hops, None, None, False, False
        self.move = None

    def request(self):
        try:
            return self.hops.send(self.got) if self.begun else next(self.hops)
        except StopIteration as stop:
            self.value, self.done = stop.value, True
            return None
        finally:
            self.begun = True


class Move:
    def __init__(self, bit, members, got):
        self.bit, self.members, self.got = bit, members, got

    def settle(self, got):
        start = 0
        for chain, a in self.members:
            chain.move = None
            if len(self.members) == 1:
                chain.got = got
            elif self.bit == "patch":
                chain.got = got[start : start + a.shape[0]]
                start += a.shape[0]
            else:
                n = a.size // 128
                chain.got = got[start : start + n].reshape(a.shape)
                start += n


class Stage:
    def __init__(self, links):
        self.links = links

    def start(self, *chains):
        wanted = {}
        for chain in chains:
            if chain.done or chain.move is not None:
                continue
            request = chain.request()
            if request is not None:
                wanted.setdefault(request[0], []).append((chain, request[1]))
        for bit, members in wanted.items():
            arrays = [a for _, a in members]
            if bit == "patch":
                sent = arrays[0] if len(arrays) == 1 else jnp.concatenate(arrays, axis=0)
                got = lax.all_to_all(sent, "patch", 1, 1, tiled=True)
            elif len(arrays) == 1:
                got = self.links.swap(arrays[0], bit)
            else:
                sent = jnp.concatenate([a.reshape(-1, 128) for a in arrays], axis=0)
                got = self.links.swap(sent, bit)
            move = Move(bit, members, got)
            for chain, _ in members:
                chain.move = move

    def join(self, values, *chains):
        moves = []
        for chain in chains:
            if chain.move is not None and chain.move not in moves:
                moves.append(chain.move)
        held, values = lax.optimization_barrier(([m.got for m in moves], values))
        for move, got in zip(moves, held):
            move.settle(got)
        return values


class Links:
    def __init__(self, batches, patches):
        self.batches, self.patches = batches, patches
        self.patch = lax.axis_index("patch")
        self.batch = lax.axis_index("batch")
        self.bits = {"c": [("p", 1)], "y": [("b", 1)], "x": [], "z": []}
        bit = 2
        while bit < patches:
            self.bits["x"].append(("p", bit))
            bit *= 2
        bit = 2
        while bit < batches:
            self.bits["z"].append(("b", bit))
            bit *= 2

    def swap(self, a, bit):
        axis, step = bit
        step = step if axis == "p" else step * self.patches
        n = self.batches * self.patches
        return lax.ppermute(a, AXES, [(i, i ^ step) for i in range(n)])

    def swap_patch(self, a, bit):
        return self.swap(a, ("p", bit))

    def mine(self, bit):
        axis, step = bit
        return ((self.patch if axis == "p" else self.batch) // step) & 1

    def expand(self, order):
        if not isinstance(order, str):
            return order
        bits = []
        for axis in order:
            one = self.bits[axis.lower()]
            bits += one if axis.islower() else one[::-1]
        return bits

    def hops(self, a, axes, order, back, trade, layout):
        names = list(self.expand(axes))
        blocks, rows, _ = a.shape
        a = a.reshape((blocks,) + (2,) * len(names) + (rows // 2 ** len(names), 128))
        layout = self.expand(layout)
        for bit in self.expand(order):
            at = names.index(bit) + 1
            names.pop(at - 1)
            got = yield bit, lax.dynamic_index_in_dim(a, 1 - self.mine(bit), at, keepdims=False)
            keep = lax.dynamic_index_in_dim(a, self.mine(bit), at, keepdims=False)
            a = (keep.astype(F32) + got.astype(F32)).astype(BF)
        if trade is not None and trade != "patch":
            bit = ("p", 1)
            size = a.shape[1:]
            pairs = a[:trade].reshape((trade // 2, 2) + size)
            got = yield bit, lax.dynamic_index_in_dim(pairs, 1 - self.mine(bit), 1, keepdims=False)
            own = lax.dynamic_index_in_dim(pairs, self.mine(bit), 1, keepdims=False)
            a = jnp.concatenate([self.join(own, got, bit, 0).reshape((trade,) + size), a[trade:]])
        if trade == "patch":
            a = a.reshape((blocks, self.patches) + a.shape[-2:])
            a = yield "patch", a
            a = a.reshape((blocks * self.patches,) + a.shape[-2:])
        have = []
        for bit in self.expand(back):
            got = yield bit, a
            at = 1 + sum(layout.index(other) < layout.index(bit) for other in have)
            have.append(bit)
            a = self.join(a, got, bit, at)
        return a.reshape(a.shape[0], -1, 128)

    def join(self, a, got, bit, at):
        return jnp.where(
            self.mine(bit) == 0, jnp.stack([a, got], axis=at), jnp.stack([got, a], axis=at)
        )

    def chain(self, a, axes, order, back, trade=None, layout="yz"):
        return Chain(self.hops(a, axes, order, back, trade, layout))

    def apart(self, a):
        got = {0: a}
        bit = self.patches // 2
        while bit > 1:
            for j in sorted(got):
                got[j | bit] = self.swap_patch(got[j], bit)
            bit //= 2
        return got

    def items(self, a):
        got = self.apart(a)
        for j in sorted(got):
            got[j | 1] = self.swap_patch(got[j], 1)
        return got

    def deal(self, parts):
        return [parts[0]] + [self.swap_patch(parts[j], j) for j in range(1, self.patches)]


def assemble_kernel(count, order, valid, *refs):
    out = refs[count]
    pieces = [refs[n][b][:, :valid].astype(F32) for n, b in order]
    out[...] = jnp.concatenate(pieces, axis=1)


def assemble(parts, order, valid=128):
    rows = parts[0].shape[1]
    step = min(rows, 128)
    return pl.pallas_call(
        functools.partial(assemble_kernel, len(parts), order, valid),
        grid=(rows // step,),
        in_specs=[pl.BlockSpec((a.shape[0], step, 128), lambda i: (0, i, 0)) for a in parts],
        out_specs=pl.BlockSpec((step, len(order) * valid), lambda i: (i, 0)),
        out_shape=jax.ShapeDtypeStruct((rows, len(order) * valid), F32),
        compiler_params=params("arbitrary"),
        cost_estimate=cost(2),
        name="assemble",
    )(*parts)


def pieces_kernel(steps, a_ref, out):
    piece = pl.program_id(0) // steps
    blocks = a_ref.shape[0] // 2

    def put(n):
        for b in range(blocks):
            out[:, b * 128 : (b + 1) * 128] = a_ref[2 * b + n].astype(F32)

    for n in range(2):
        pl.when(piece == n)(functools.partial(put, n))


def pieces_call(a):
    blocks, rows, _ = a.shape
    step = min(rows, 128)
    steps = rows // step
    return pl.pallas_call(
        functools.partial(pieces_kernel, steps),
        grid=(2 * steps,),
        in_specs=[pl.BlockSpec((blocks, step, 128), lambda i: (0, i % steps, 0))],
        out_specs=pl.BlockSpec((step, blocks * 64), lambda i: (i, 0)),
        out_shape=jax.ShapeDtypeStruct((2 * rows, blocks * 64), F32),
        compiler_params=params("arbitrary"),
        cost_estimate=cost(4),
        name="pieces",
    )(a)


def tables(code, times):
    head = 64
    half = head // 6
    band = 2 * half
    dims = jnp.arange(head)
    freq = jnp.power(THETA, -2.0 * (dims % half).astype(F32) / band)
    places = jnp.stack([times, (code // GRID).astype(F32), (code % GRID).astype(F32)], axis=-1)
    which = jnp.minimum(dims // band, 2)
    pick = jnp.where(
        which == 0, places[..., 0:1], jnp.where(which == 1, places[..., 1:2], places[..., 2:3])
    )
    angle = pick * freq
    turned = dims < 3 * band
    cos = jnp.where(turned, jnp.cos(angle), 1.0)
    sin = jnp.where(turned, jnp.sin(angle) * jnp.where(dims % band < half, -1.0, 1.0), 0.0)
    return jnp.concatenate([cos, cos, sin, sin], axis=-1)


def per_device(
    batches, patches, tokens, cotangent, episode_frames, kinds, patch_pos,
    ln1_gain, ln1_shift, w_qkv, w_out, ln2_gain, ln2_shift, w_up, w_down,
):
    tokens = tokens[0]
    frames, width, dim = tokens.shape
    rows = frames * width
    local = dim // patches
    links = Links(batches, patches)
    me = links.patch
    core = me & 1
    gain1, shift1, gain2, shift2 = (
        a.astype(F32).reshape(1, dim) for a in (ln1_gain, ln1_shift, ln2_gain, ln2_shift)
    )
    dy = cotangent.reshape(rows, dim)

    code = jnp.where(kinds[0] == 0, patch_pos[0], 0)
    codes = links.items(code)
    codes, tokens, dy = lax.optimization_barrier((codes, tokens, dy))
    mate = links.swap_patch(tokens, 1)
    dy_mate = links.swap_patch(dy, 1)
    apart = links.apart(tokens)
    ends = jnp.cumsum(episode_frames[0])
    frame_ids = jnp.arange(frames, dtype=jnp.int32)
    starts = jnp.max(
        jnp.where(ends[None, :] <= frame_ids[:, None], ends[None, :], 0), axis=1
    )
    info = jnp.concatenate([me[None], starts]).astype(jnp.int32)
    pad = max(128, local)
    pairs = pad // 128
    valid = min(128, local)
    columns = []
    for p in range(pairs):
        for n in range(3):
            at = n * dim + me * local + p * 128
            columns.append(lax.dynamic_slice(w_qkv, (jnp.int32(0), at), (dim, valid)))
            if valid < 128:
                columns.append(jnp.zeros((dim, 128 - valid), BF))
    w_local = jnp.concatenate(columns, axis=1)

    members = [[0, 1], list(range(2, patches))]
    css = []
    for group in members:
        place = jnp.concatenate([codes[j] for j in group], axis=1)
        times = jnp.broadcast_to(frame_ids.astype(F32)[:, None], place.shape)
        css.append(tables(place, times))
    near = qkv_call([tokens, mate], css[0], w_local, gain1, shift1)
    dg = pre_call(info, dy, dy_mate, w_down, patches)
    near, dg, apart, css = lax.optimization_barrier((near, dg, apart, css))
    far_items = []
    for j in range(2, patches, 2):
        far_items += [apart[j], links.swap_patch(apart[j], 1)]
    far = qkv_call(far_items, css[1], w_local, gain1, shift1)
    hs, qkvs = [near[0], far[0]], [near[1], far[1]]

    *o_send, o_full, lse = attend_call(info, qkvs, patches)
    o_in = links.deal([a[..., :local] for a in o_send])
    x1, h2, o_own = project_call(info, o_in, tokens, w_out, gain2, shift2)
    h2_mate = links.swap_patch(h2, 1)
    o_mate = links.swap_patch(o_own, 1)
    stage = Stage(links)
    g, du, dw0, dw1, dh_own, dh_mate = ffn_call(
        info, h2, h2_mate, dy, dy_mate, dg, w_up, patches
    )
    inner, outer = links.bits["z"][:1], links.bits["z"][1:]
    ys, xs = links.bits["y"], links.bits["x"]

    def two_pieces(a):
        return a.reshape(a.shape[0] * 2, a.shape[1] // 2, 128)

    def step(held, *chains):
        held = stage.join(held, *chains)
        for chain in chains:
            stage.start(chain)
        return held

    def finish(held, *chains):
        while not all(c.done for c in chains):
            held = step(held, *chains)
        return held

    d1 = links.chain(two_pieces(dw0), "Xyz", ys + inner, "")
    d2 = links.chain(two_pieces(dw1), "Xyz", inner + ys, "")
    stage.start(d1)
    stage.start(d2)
    dh_recv = links.swap_patch(dh_mate, 1)
    dx1, da, sums2, *d_o = mid_call(
        info, dh_own, dh_recv, x1, dy, w_out, gain2, frames, patches
    )
    d_o, du, da, o_mate = lax.optimization_barrier((d_o, du, da, o_mate))
    da_mate = links.swap_patch(da, 1)
    do_in = links.deal(d_o)
    sides = (o_own, o_mate, da, da_mate)
    dw1 = up_call(info, h2, h2_mate, du, *sides, patches, 0)
    dw2 = up_call(info, h2, h2_mate, du, *sides, patches, 1)
    do_in, dw1, dw2 = step((do_in, dw1, dw2), d1, d2)
    u1 = links.chain(dw1, "Xcyz", xs + inner + ys, "")
    u2 = links.chain(dw2, "Xcyz", ys + xs + inner, "")
    stage.start(u1)
    if pad > local:
        do_in = [jnp.pad(a, ((0, 0), (0, 0), (0, pad - local))) for a in do_in]
    dqkv = attend_back_call(info, qkvs, css, do_in, o_full, lse, patches, 0)
    dwq = [dwq_call(hs, dqkv)]
    dqkv, dwq, do_in = step((dqkv, dwq, do_in), d1, d2)
    dqkv = finish(dqkv, d1, d2)
    dqkvs = [dqkv]
    d = links.chain(
        jnp.concatenate([d1.value, d2.value], axis=0),
        xs[::-1] + outer,
        outer + xs,
        outer[::-1] + inner + ys,
    )
    stage.start(d)
    stage.start(u2)
    for pair in range(1, pairs):
        dqkvs.append(attend_back_call(info, qkvs, css, do_in, o_full, lse, patches, pair))
    for one in dqkvs[1:]:
        dwq.append(dwq_call(hs, one))
    even, odd = dh_call(dqkvs, w_local, patches)
    odd, even, dwq, g = step((odd, even, dwq, g), u1, d, u2)
    odd = links.swap_patch(odd, 1)
    q = links.chain(jnp.concatenate(dwq, axis=0), "Xcyz", "yz", "zy", "patch")
    stage.start(q)
    slots = (even.astype(F32) + odd.astype(F32)).astype(BF)
    bit = patches // 2
    while bit > 2:
        n = slots.shape[0] // 2
        slots = (slots[:n].astype(F32) + links.swap_patch(slots[n:], bit).astype(F32)).astype(BF)
        bit //= 2
    got = links.swap_patch(slots[1], 2)
    out_own, out_mate = down_call(info, x1, g, w_down, patches)
    out_own, out_mate, sums2 = step((out_own, out_mate, sums2), d)
    out_recv = links.swap_patch(out_mate, 1)
    sums2 = step(sums2, u1)
    sums2 = step(sums2, d)
    sums2 = step(sums2, u2)
    sums2, out_own, out_recv = step((sums2, out_own, out_recv), q)
    out = (out_own + out_recv.astype(F32)).astype(BF)
    sums2 = step(sums2, u1, u2)
    sums2 = finish(sums2, u1, u2)
    w = jnp.concatenate([u1.value, u2.value], axis=0)
    w = w.reshape(2 * w.shape[0], -1, 128)
    w = links.chain(w, outer, outer, outer[::-1] + ys + inner, w.shape[0])
    stage.start(w)
    sums2 = step(sums2, q)
    sums2 = step(sums2, d)
    slots, got, sums2 = lax.optimization_barrier((slots, got, sums2))
    grad_tokens, sums1 = last_call(
        slots[0].reshape(rows, dim), got.reshape(rows, dim), tokens.reshape(rows, dim), dx1, gain1
    )
    sums = jnp.concatenate([sums1, sums2], axis=0)
    sums = step(sums, w)
    sums = sums.reshape(4, patches, local).transpose(1, 0, 2)
    sums = jnp.broadcast_to(sums[None], (batches,) + sums.shape)
    sums = lax.all_to_all(sums.reshape((-1,) + sums.shape[2:]), AXES, 0, 0, tiled=True)
    grad_tokens, sums = step((grad_tokens, sums), q)
    sums = jnp.sum(sums, axis=0)
    grad_tokens = step(grad_tokens, w)
    grad_tokens = step(grad_tokens, d)
    grad_tokens = step(grad_tokens, q)
    grad_tokens = step(grad_tokens, q)
    grad_tokens = step(grad_tokens, w)
    grad_tokens = step(grad_tokens, q)
    grad_tokens = step(grad_tokens, w)
    grad_tokens = step(grad_tokens, q)
    grad_tokens = finish(grad_tokens, q)
    grad_tokens = finish(grad_tokens, w)
    grad_tokens = finish(grad_tokens, d)
    down = pieces_call(d.value)

    nx = patches // 2
    each = dw1.shape[0]
    per = (each - dim // 512) // nx
    ups, wos = [], []
    for owner in range(2):
        for n in range(2):
            at = (owner * 2 + n) * each
            wos += [(0, at + nx * per + t) for t in range(dim // 512)]
    for i in range(nx):
        for owner in range(2):
            for n in range(2):
                ups += [(0, (owner * 2 + n) * each + i * per + t) for t in range(per)]
    up = assemble([w.value], ups)
    grad_wo = assemble([w.value], wos)
    order = []
    for n in range(3):
        for p in range(patches):
            order += [(0, (pair * 3 + n) * patches + p) for pair in range(pairs)]
    qkv = assemble([q.value], order, valid)

    return (
        out.reshape(1, frames, width, dim),
        grad_tokens.reshape(1, frames, width, dim),
        sums[0],
        sums[1],
        qkv,
        grad_wo,
        sums[2],
        sums[3],
        up,
        down,
    )


def solution(mesh):
    placed = (
        P("batch", None, "patch", None),
        P("batch", None, "patch", None),
        P("batch", None),
        P("batch", None, "patch"),
        P("batch", None, "patch"),
    ) + (P(),) * 8
    return jax.shard_map(
        functools.partial(per_device, mesh.shape["batch"], mesh.shape["patch"]),
        mesh=mesh,
        in_specs=placed,
        out_specs=(
            P("batch", None, "patch", None),
            P("batch", None, "patch", None),
            P("patch"),
            P("patch"),
            P("patch", None),
            P("patch", None),
            P("patch"),
            P("patch"),
            P("patch", None),
            P("patch", None),
        ),
        check_vma=False,
    )
```

time: 421 us -> 386 us (0.917)
  waiting for transfers between devices: 115 us -> 138 us
  local copies, waits for them, and re-layouts: 39.3 us -> 20 us
  other arithmetic: 44.4 us -> 27.5 us
  starting transfers between devices: 60 us -> 43.4 us
    ppermute x53 -> x46, waiting for transfers between devices: 106 us -> 124 us  [swap(): return lax.ppermute(a, AXES, [(i, i ^ step) for i in range(n)])]
    ppermute x53 -> x46, starting transfers between devices: 49.3 us -> 35.9 us  [swap(): return lax.ppermute(a, AXES, [(i, i ^ step) for i in range(n)])]
    slice x35 -> x0, local copies, waits for them, and re-layouts: 9.77 us -> none  [the longest x31 6.76 us: close(): chain.got = got[start:start + n].reshape(a.shape)]
    concatenate x16 -> x2, other arithmetic: 7.26 us -> 0.2 us  [the longest x1 0.14 us: per_device(): q = links.chain(jnp.concatenate(dwq, axis=0), 'Xcyz', 'yz', 'zy', 'patch')]
    convert_element_type x36 -> x16, other arithmetic: 14.7 us -> 8.7 us  [hops(): a = (keep.astype(F32) + got.astype(F32)).astype(BF)]
    all_to_all x3 -> x2, waiting for transfers between devices: 9.18 us -> 13.7 us  [the longest x1 10.7 us: per_device(): lax.all_to_all(sums.reshape((-1,) + sums.shape[2:]), AXES, 0, 0, tiled=True)]
    unnamed x136 -> x57, local copies, waits for them, and re-layouts: 13.4 us -> 9.73 us
    pallas_call x4 -> x3, Pallas kernels: 8.89 us -> 5.47 us  [assemble(): pl.pallas_call(functools.partial(assemble_kernel, len(parts), order, vali...]
  transfers between devices with their start and end apart: 56 -> 48, of which waited for: 22 -> 20; matrix products, arithmetic and copies ran while one was open for 12% -> 11% of each run, Pallas kernels for 21% -> 26%
where the time goes in v1:
time: 386 us; the launch traced here: 380 us
  Pallas kernels  150 us (39%)
  waiting for transfers between devices  138 us (36%)
  starting transfers between devices  43.4 us (11%)
  other arithmetic  27.5 us (7%)
  local copies, waits for them, and re-layouts  20 us (5%)
    ppermute x46, waiting for transfers between devices, swap(): return lax.ppermute(a, AXES, [(i, i ^ step) for i in range(n)])  124 us
    ppermute x46, starting transfers between devices, swap(): return lax.ppermute(a, AXES, [(i, i ^ step) for i in range(n)])  35.9 us
    pallas_call x2, Pallas kernels, attend_back_call(): pl.pallas_call(functools.partial(attend_back_kernel, groups, pair, patche...  30.7 us
    pallas_call x1, Pallas kernels, ffn_call(): pl.pallas_call(ffn_kernel, grid_spec=pltpu.PrefetchScalarGridSpec(num_sca...  23.9 us
    pallas_call x1, Pallas kernels, attend_call(): pl.pallas_call(functools.partial(attend_kernel, groups, local, patches, f...  13.9 us
    pallas_call x2, Pallas kernels, up_call(): pl.pallas_call(kernel, grid_spec=pltpu.PrefetchScalarGridSpec(num_scalar_...  13.6 us
    pallas_call x2, Pallas kernels, qkv_call(): pl.pallas_call(functools.partial(qkv_kernel, count, local), grid=(frames...  13.4 us
    all_to_all x1, waiting for transfers between devices, per_device(): lax.all_to_all(sums.reshape((-1,) + sums.shape[2:]), AXES, 0, 0, tiled=True)  10.7 us
  transfers between devices with their start and end apart: 48, of which 20 were waited for; matrix products, arithmetic and copies ran while one was open for 11% of the time, Pallas kernels for 26%

profile of v1, /device:TPU:0, one launch (start us, length us, event | category | flops | bytes accessed | tf_op | source)
XLA Modules:
  0.0 380.5 jit_solution(6183429469675195953)
XLA Ops:
  22.8 7.3 %qkv.2 = (bf16[8,128,1024]{2,1,0:T(8,128)(2,1)}, bf16[8,128,768]{2,1,0:T(8,128)(2,1)}) custom-call(bf16[8,64,1024]{2,1,0:T(8,128)(2,1)S(1)} %bitcast.176, bf16[8,64,1024]{2,1,0:T(8,128)(2,1)} %collective-permute-done.3.refs_1_, f32[8,128,256]{2,1,0:T(8,128)S(1)} %pad_maximum_fusion.4.refs_2_, ...), custom_call_target="tpu_custom_call" | custom-call | flops 1581250048 | bytes 1 | tf_op jit(solution)/shard_map/qkv/pallas_call | solution.py:123
  30.1 6.7 %pre.1.dg_ref = bf16[1024,2048]{1,0:T(8,128)(2,1)} custom-call(s32[9]{0:T(128)S(1)} %pad_add_fusion.2.info_ref, bf16[512,1024]{1,0:T(8,128)(2,1)S(1)} %bitcast.182, bf16[512,1024]{1,0:T(8,128)(2,1)S(1)} %collective-permute-done.4.dy_mate, bf16[4096,1024]{1,0:T(8,128)(2,1)S(1)} %copy-done), custom_call_target="tpu_custom_call" | custom-call | flops 2443749888 | bytes 1 | tf_op jit(solution)/shard_map/pre/pallas_call | solution.py:422
  36.9 6.2 %collective-permute-done.5.refs_0_ = bf16[8,64,1024]{2,1,0:T(8,128)(2,1)S(1)} collective-permute-done((bf16[8,64,1024]{2,1,0:T(8,128)(2,1)S(1)}, bf16[8,64,1024]{2,1,0:T(8,128)(2,1)S(1)}, u32[]{:S(2)}, u32[]{:S(2)}) %collective-permute-start.5) | collective-permute-done | bytes 1048608 | tf_op jit(solution)/shard_map/ppermute | solution.py:871
  45.7 6.1 %qkv.3 = (bf16[8,128,1024]{2,1,0:T(8,128)(2,1)}, bf16[8,128,768]{2,1,0:T(8,128)(2,1)}) custom-call(bf16[8,64,1024]{2,1,0:T(8,128)(2,1)S(1)} %collective-permute-done.5.refs_0_, bf16[8,64,1024]{2,1,0:T(8,128)(2,1)S(1)} %collective-permute-done.6.refs_1_, f32[8,128,256]{2,1,0:T(8,128)S(1)} %pad_maximum_fusion.5.refs_2_.refs_3_, ...), custom_call_target="tpu_custom_call" | custom-call | flops 1581250048 | bytes 1 | tf_op jit(solution)/shard_map/qkv/pallas_call | solution.py:123
  51.9 13.9 %attend.1 = (bf16[8,64,256]{2,1,0:T(8,128)(2,1)S(1)}, bf16[8,64,256]{2,1,0:T(8,128)(2,1)S(1)}, bf16[8,64,256]{2,1,0:T(8,128)(2,1)S(1)}, bf16[8,64,256]{2,1,0:T(8...) custom-call(s32[9]{0:T(128)S(1)} %pad_add_fusion.2.info_ref, ...), custom_call_target="tpu_custom_call" | custom-call | flops 3593750016 | bytes 1 | tf_op jit(solution)/shard_map/attend/pallas_call | solution.py:240
  67.7 7.4 %collective-permute-done.8.refs_2_ = bf16[8,64,256]{2,1,0:T(8,128)(2,1)S(1)} collective-permute-done((bf16[8,64,256]{2,1,0:T(8,128)(2,1)S(1)}, bf16[8,64,256]{2,1,0:T(8,128)(2,1)S(1)}, u32[]{:S(2)}, u32[]{:S(2)}) %collective-permute-start.8) | collective-permute-done | bytes 262176 | tf_op jit(solution)/shard_map/ppermute | solution.py:871
  75.1 4.5 %collective-permute-done.9.refs_3_ = bf16[8,64,256]{2,1,0:T(8,128)(2,1)S(1)} collective-permute-done((bf16[8,64,256]{2,1,0:T(8,128)(2,1)S(1)}, bf16[8,64,256]{2,1,0:T(8,128)(2,1)S(1)}, u32[]{:S(2)}, u32[]{:S(2)}) %collective-permute-start.9) | collective-permute-done | bytes 262176 | tf_op jit(solution)/shard_map/ppermute | solution.py:871
  85.9 23.9 %ffn.1 = (bf16[1024,2048]{1,0:T(8,128)(2,1)}, bf16[1024,2048]{1,0:T(8,128)(2,1)}, bf16[4,2048,128]{2,1,0:T(8,128)(2,1)}, bf16[4,2048,128]{2,1,0:T(8,128)(2,1)}, ...) custom-call(s32[9]{0:T(128)S(1)} %pad_add_fusion.2.info_ref, bf16[512,1024]{1,0:T(8,128)(2,1)S(1)} %get-tuple-element.153.h_own.refs_0_, ...), custom_call_target="tpu_custom_call" | custom-call | flops 7187500032 | bytes 1 | tf_op jit(solution)/shard_map/ffn/pallas_call | solution.py:482
  112.8 6.8 %mid.1 = (f32[512,1024]{1,0:T(8,128)}, bf16[512,1024]{1,0:T(8,128)(2,1)S(1)}, f32[2,1024]{1,0:T(2,128)S(1)}, bf16[8,64,256]{2,1,0:T(8,128)(2,1)S(1)}, bf16[8,64,...) custom-call(s32[9]{0:T(128)S(1)} %pad_add_fusion.2.info_ref, ...), custom_call_target="tpu_custom_call" | custom-call | flops 1724999936 | bytes 1 | tf_op jit(solution)/shard_map/mid/pallas_call | solution.py:650
  128.9 6.7 %up.3 = bf16[10,1024,128]{2,1,0:T(8,128)(2,1)S(1)} custom-call(s32[9]{0:T(128)S(1)} %pad_add_fusion.2.info_ref, bf16[512,1024]{1,0:T(8,128)(2,1)} %copy-done.2, bf16[512,1024]{1,0:T(8,128)(2,1)} %copy-done.3, bf16[1024,2048]{1,0:T(8,128)(2,1)} %get-tuple-element.171.refs_2_, bf16[512,1024]{1,0:T(8,128)(2,1)} %get-tuple-element.166.refs_3_, ...), custom_call_target="tpu_custom_call" | custom-call | flops 1724999936 | bytes 1 | tf_op jit(solution)/shard_map/up/pallas_call | solution.py:543
  135.6 6.9 %up.2 = bf16[10,1024,128]{2,1,0:T(8,128)(2,1)S(1)} custom-call(s32[9]{0:T(128)S(1)} %pad_add_fusion.2.info_ref, bf16[512,1024]{1,0:T(8,128)(2,1)} %copy-done.2, bf16[512,1024]{1,0:T(8,128)(2,1)} %copy-done.3, bf16[1024,2048]{1,0:T(8,128)(2,1)} %get-tuple-element.171.refs_2_, bf16[512,1024]{1,0:T(8,128)(2,1)} %get-tuple-element.166.refs_3_, ...), custom_call_target="tpu_custom_call" | custom-call | flops 1724999936 | bytes 1 | tf_op jit(solution)/shard_map/up/pallas_call | solution.py:543
  142.6 4.9 %collective-permute-done.12 = bf16[8,2,2,2,64,128]{5,4,0,1,3,2:T(8,128)(2,1)} collective-permute-done((bf16[8,2,2,2,64,128]{5,4,0,1,3,2:T(8,128)(2,1)}, bf16[8,2,2,2,64,128]{5,4,0,1,3,2:T(8,128)(2,1)}, u32[]{:S(2)}, u32[]{:S(2)}) %collective-permute-start.12) | collective-permute-done | bytes 1048608 | tf_op jit(solution)/shard_map/ppermute | solution.py:871
  159.2 15.4 %attend_back.2 = (bf16[8,128,384]{2,1,0:T(8,128)(2,1)S(1)}, bf16[8,128,384]{2,1,0:T(8,128)(2,1)S(1)}) custom-call(s32[9]{0:T(128)S(1)} %pad_add_fusion.2.info_ref, bf16[8,128,768]{2,1,0:T(8,128)(2,1)} %get-tuple-element.145.refs_0_, bf16[8,128,768]{2,1,0:T(8,128)(2,1)} %get-tuple-element.148.refs_1_, f32[8,128,256]{2,1,0:T(8,128)} %copy-done.9, ...), custom_call_target="tpu_custom_call" | custom-call | flops 4312500224 | bytes 1 | tf_op jit(solution)/shard_map/attend_back/pallas_call | solution.py:327
  182.1 15.3 %attend_back.3 = (bf16[8,128,384]{2,1,0:T(8,128)(2,1)S(1)}, bf16[8,128,384]{2,1,0:T(8,128)(2,1)S(1)}) custom-call(s32[9]{0:T(128)S(1)} %pad_add_fusion.2.info_ref, bf16[8,128,768]{2,1,0:T(8,128)(2,1)} %get-tuple-element.145.refs_0_, bf16[8,128,768]{2,1,0:T(8,128)(2,1)} %get-tuple-element.148.refs_1_, f32[8,128,256]{2,1,0:T(8,128)} %copy-done.9, ...), custom_call_target="tpu_custom_call" | custom-call | flops 4312500224 | bytes 1 | tf_op jit(solution)/shard_map/attend_back/pallas_call | solution.py:327
  197.5 4.4 %dwq.3 = bf16[3,1024,128]{2,1,0:T(8,128)(2,1)S(1)} custom-call(bf16[8,128,1024]{2,1,0:T(8,128)(2,1)} %get-tuple-element.186.refs_0_, bf16[8,128,1024]{2,1,0:T(8,128)(2,1)} %get-tuple-element.187.refs_1_, bf16[8,128,384]{2,1,0:T(8,128)(2,1)S(1)} %get-tuple-element.197.refs_2_, bf16[8,128,384]{2,1,0:T(8,128)(2,1)S(1)} %get-tuple-element.198.refs_3_), custom_call_target="tpu_custom_call" | custom-call | flops 1236249984 | bytes 1 | tf_op jit(solution)/shard_map/dwq/pallas_call | solution.py:697
  201.8 5.8 %dh.1 = (bf16[2,8,64,1024]{3,2,1,0:T(8,128)(2,1)S(1)}, bf16[2,8,64,1024]{3,2,1,0:T(8,128)(2,1)S(1)}) custom-call(bf16[8,128,384]{2,1,0:T(8,128)(2,1)S(1)} %get-tuple-element.191.refs_2_.refs_0_, bf16[8,128,384]{2,1,0:T(8,128)(2,1)S(1)} %get-tuple-element.192.refs_3_.refs_1_, bf16[8,128,384]{2,1,0:T(8,128)(2,1)S(1)} %get-tuple-element.197.refs_2_, ...), custom_call_target="tpu_custom_call" | custom-call | flops 1437500032 | bytes 1 | tf_op jit(solution)/shard_map/dh/pallas_call | solution.py:733
  212.5 9.3 %down.1 = (f32[512,1024]{1,0:T(8,128)S(1)}, bf16[512,1024]{1,0:T(8,128)(2,1)S(1)}) custom-call(s32[9]{0:T(128)S(1)} %pad_add_fusion.2.info_ref, f32[512,1024]{1,0:T(8,128)} %get-tuple-element.159.x1_ref, bf16[1024,2048]{1,0:T(8,128)(2,1)} %get-tuple-element.207.g0_ref.g1_ref, bf16[1024,2048]{1,0:T(8,128)(2,1)} %get-tuple-element.207.g0_ref.g1_ref, ...), custom_call_target="tpu_custom_call" | custom-call | flops 2443749888 | bytes 1 | tf_op jit(solution)/shard_map/down/pallas_call | solution.py:590
  224.0 13.2 %collective-permute-done.27 = bf16[16,64,128]{2,1,0:T(8,128)(2,1)S(1)} collective-permute-done((bf16[16,64,128]{2,1,0:T(8,128)(2,1)S(1)}, bf16[16,64,128]{2,1,0:T(8,128)(2,1)S(1)}, u32[]{:S(2)}, u32[]{:S(2)}) %collective-permute-start.27) | collective-permute-done | bytes 262176 | tf_op jit(solution)/shard_map/ppermute | solution.py:871
  254.9 18.7 %collective-permute-done.36 = bf16[6,2,2,2,32,128]{5,4,3,2,1,0:T(8,128)(2,1)S(1)} collective-permute-done((bf16[6,2,2,2,32,128]{5,4,3,2,1,0:T(8,128)(2,1)S(1)}, bf16[6,2,2,2,32,128]{5,4,3,2,1,0:T(8,128)(2,1)S(1)}, u32[]{:S(2)}, u32[]{:S(2)}) %collective-permute-start.36) | collective-permute-done | bytes 393248 | tf_op jit(solution)/shard_map/ppermute | solution.py:871
  289.9 10.7 %all-to-all-done = f32[32,4,256]{2,1,0:T(4,128)S(1)} async-done(((f32[32,4,256]{2,1,0:T(4,128)}), f32[32,4,256]{2,1,0:T(4,128)S(1)}, u32[]{:S(2)}, u32[]{:S(2)}) %all-to-all-start) | async-done | bytes 131104 | tf_op jit(solution)/shard_map/all_to_all | solution.py:1167
  312.6 11.9 %collective-permute-done.41 = bf16[24,32,128]{2,1,0:T(8,128)(2,1)S(1)} collective-permute-done((bf16[24,32,128]{2,1,0:T(8,128)(2,1)S(1)}, bf16[24,32,128]{2,1,0:T(8,128)(2,1)S(1)}, u32[]{:S(2)}, u32[]{:S(2)}) %collective-permute-start.41) | collective-permute-done | bytes 196640 | tf_op jit(solution)/shard_map/ppermute | solution.py:871
  327.0 17.7 %collective-permute-done.43 = bf16[24,2,32,128]{3,2,0,1:T(8,128)(2,1)S(1)} collective-permute-done((bf16[24,2,32,128]{3,2,0,1:T(8,128)(2,1)S(1)}, bf16[24,2,32,128]{3,2,0,1:T(8,128)(2,1)S(1)}, u32[]{:S(2)}, u32[]{:S(2)}) %collective-permute-start.43) | collective-permute-done | bytes 393248 | tf_op jit(solution)/shard_map/ppermute | solution.py:871
  352.4 12.8 %collective-permute-done.45 = bf16[24,2,2,32,128]{4,3,0,1,2:T(8,128)(2,1)S(1)} collective-permute-done((bf16[24,2,2,32,128]{4,3,0,1,2:T(8,128)(2,1)S(1)}, bf16[24,2,2,32,128]{4,3,0,1,2:T(8,128)(2,1)S(1)}, u32[]{:S(2)}, u32[]{:S(2)}) %collective-permute-start.45) | collective-permute-done | bytes 786464 | tf_op jit(solution)/shard_map/ppermute | solution.py:871
  367.9 8.3 %collective-permute-done.44 = bf16[40,2,2,32,128]{4,3,2,1,0:T(8,128)(2,1)S(1)} collective-permute-done((bf16[40,2,2,32,128]{4,3,2,1,0:T(8,128)(2,1)S(1)}, bf16[40,2,2,32,128]{4,3,2,1,0:T(8,128)(2,1)S(1)}, u32[]{:S(2)}, u32[]{:S(2)}) %collective-permute-start.44) | collective-permute-done | bytes 1310752 | tf_op jit(solution)/shard_map/ppermute | solution.py:871
  (236 shorter events, 133.7 us)
Async XLA Ops:
  17.7 25.4 %collective-permute-start.5 = (bf16[8,64,1024]{2,1,0:T(8,128)(2,1)S(1)}, bf16[8,64,1024]{2,1,0:T(8,128)(2,1)S(1)}, u32[]{:S(2)}, u32[]{:S(2)}) collective-permute-start(bf16[8,64,1024]{2,1,0:T(8,128)(2,1)S(1)} %bitcast.175), channel_id=1, source_target_pairs={{0,2},{1,3},{2,0},{3,1},{4,6},{5,7},{6,4},{7,5},{8,10},{9,11},{10,... | collective-permute-start | bytes 3145736 | tf_op jit(solution)/shard_map/ppermute | solution.py:871
  121.7 25.7 %collective-permute-start.12 = (bf16[8,2,2,2,64,128]{5,4,0,1,3,2:T(8,128)(2,1)}, bf16[8,2,2,2,64,128]{5,4,0,1,3,2:T(8,128)(2,1)}, u32[]{:S(2)}, u32[]{:S(2)}) collective-permute-start(bf16[8,2,2,2,64,128]{5,4,0,1,3,2:T(8,128)(2,1)} %bitcast.163), channel_id=1, source_target_pairs={{0,8},{1,9},{2,10},{3,11},{4,12},{5,13},{6,14},{7,15},{8,0},{9,1},... | collective-permute-start | bytes 3145736 | tf_op jit(solution)/shard_map/ppermute | solution.py:871
  125.7 25.5 %collective-permute-start.11 = (bf16[8,2,2,2,64,128]{5,4,0,1,3,2:T(8,128)(2,1)}, bf16[8,2,2,2,64,128]{5,4,0,1,3,2:T(8,128)(2,1)}, u32[]{:S(2)}, u32[]{:S(2)}) collective-permute-start(bf16[8,2,2,2,64,128]{5,4,0,1,3,2:T(8,128)(2,1)} %bitcast.164), channel_id=1, source_target_pairs={{0,4},{1,5},{2,6},{3,7},{4,0},{5,1},{6,2},{7,3},{8,12},{9,13},{10,... | collective-permute-start | bytes 3145736 | tf_op jit(solution)/shard_map/ppermute | solution.py:871
  127.0 24.1 %collective-permute-start.15 = (bf16[8,64,256]{2,1,0:T(8,128)(2,1)S(1)}, bf16[8,64,256]{2,1,0:T(8,128)(2,1)S(1)}, u32[]{:S(2)}, u32[]{:S(2)}) collective-permute-start(bf16[8,64,256]{2,1,0:T(8,128)(2,1)S(1)} %get-tuple-element.168), channel_id=1, source_target_pairs={{0,1},{1,0},{2,3},{3,2},{4,5},{5,4},{6,7},{7,6},{8,9},{9,8},{10,11... | collective-permute-start | bytes 786440 | tf_op jit(solution)/shard_map/ppermute | solution.py:871
  127.0 24.1 %collective-permute-start.16 = (bf16[8,64,256]{2,1,0:T(8,128)(2,1)S(1)}, bf16[8,64,256]{2,1,0:T(8,128)(2,1)S(1)}, u32[]{:S(2)}, u32[]{:S(2)}) collective-permute-start(bf16[8,64,256]{2,1,0:T(8,128)(2,1)S(1)} %get-tuple-element.169), channel_id=1, source_target_pairs={{0,2},{1,3},{2,0},{3,1},{4,6},{5,7},{6,4},{7,5},{8,10},{9,11},{10,... | collective-permute-start | bytes 786440 | tf_op jit(solution)/shard_map/ppermute | solution.py:871
  127.6 23.6 %collective-permute-start.17 = (bf16[8,64,256]{2,1,0:T(8,128)(2,1)S(1)}, bf16[8,64,256]{2,1,0:T(8,128)(2,1)S(1)}, u32[]{:S(2)}, u32[]{:S(2)}) collective-permute-start(bf16[8,64,256]{2,1,0:T(8,128)(2,1)S(1)} %get-tuple-element.170), channel_id=1, source_target_pairs={{0,3},{1,2},{2,1},{3,0},{4,7},{5,6},{6,5},{7,4},{8,11},{9,10},{10,... | collective-permute-start | bytes 786440 | tf_op jit(solution)/shard_map/ppermute | solution.py:871
  152.9 26.1 %collective-permute-start.21 = (bf16[8,2,2,64,128]{4,3,0,1,2:T(8,128)(2,1)S(1)}, bf16[8,2,2,64,128]{4,3,0,1,2:T(8,128)(2,1)S(1)}, u32[]{:S(2)}, u32[]{:S(2)}) collective-permute-start(bf16[8,2,2,64,128]{4,3,0,1,2:T(8,128)(2,1)S(1)} %dynamic-slice_bitcast_fusion.5), channel_id=1, source_target_pairs={{0,4},{1,5},{2,6},{3,7},{4,0},{5,1},{6,2},{7,3},{8,12},{9,13},{10,... | collective-permute-start | bytes 1572872 | tf_op jit(solution)/shard_map/ppermute | solution.py:871
  156.0 23.0 %collective-permute-start.20 = (bf16[8,2,2,64,128]{4,3,0,1,2:T(8,128)(2,1)S(1)}, bf16[8,2,2,64,128]{4,3,0,1,2:T(8,128)(2,1)S(1)}, u32[]{:S(2)}, u32[]{:S(2)}) collective-permute-start(bf16[8,2,2,64,128]{4,3,0,1,2:T(8,128)(2,1)S(1)} %dynamic-slice_bitcast_fusion.6), channel_id=1, source_target_pairs={{0,8},{1,9},{2,10},{3,11},{4,12},{5,13},{6,14},{7,15},{8,0},{9,1},... | collective-permute-start | bytes 1572872 | tf_op jit(solution)/shard_map/ppermute | solution.py:871
  157.7 50.0 %collective-permute-start.19 = (bf16[10,2,2,2,2,32,128]{6,5,4,3,2,1,0:T(8,128)(2,1)S(1)}, bf16[10,2,2,2,2,32,128]{6,5,4,3,2,1,0:T(8,128)(2,1)S(1)}, u32[]{:S(2)}, u32[]{:S(2)}) collective-permute-start(bf16[10,2,2,2,2,32,128]{6,5,4,3,2,1,0:T(8,128)(2,1)S(1)} %dynamic-slice_bitcast_fusion.1), channel_id=1, source_target_pairs={{0,2},{1,3},{2,0},{3,1},{4,6},{5,7},{6,4},{7,5},{8,10},{9,11},{10,... | collective-permute-start | bytes 3932168 | tf_op jit(solution)/shard_map/ppermute | solution.py:871
  158.5 49.2 %collective-permute-start.23 = (bf16[10,2,2,2,2,32,128]{6,5,4,3,2,1,0:T(8,128)(2,1)S(1)}, bf16[10,2,2,2,2,32,128]{6,5,4,3,2,1,0:T(8,128)(2,1)S(1)}, u32[]{:S(2)}, u32[]{:S(2)}) collective-permute-start(bf16[10,2,2,2,2,32,128]{6,5,4,3,2,1,0:T(8,128)(2,1)S(1)} %dynamic-slice_bitcast_fusion), channel_id=1, source_target_pairs={{0,4},{1,5},{2,6},{3,7},{4,0},{5,1},{6,2},{7,3},{8,12},{9,13},{10,... | collective-permute-start | bytes 3932168 | tf_op jit(solution)/shard_map/ppermute | solution.py:871
  179.5 28.2 %collective-permute-start.22 = (bf16[16,2,64,128]{3,2,0,1:T(8,128)(2,1)S(1)}, bf16[16,2,64,128]{3,2,0,1:T(8,128)(2,1)S(1)}, u32[]{:S(2)}, u32[]{:S(2)}) collective-permute-start(bf16[16,2,64,128]{3,2,0,1:T(8,128)(2,1)S(1)} %fusion.17), channel_id=1, source_target_pairs={{0,16},{1,17},{2,18},{3,19},{4,20},{5,21},{6,22},{7,23},{8,24},{9,... | collective-permute-start | bytes 1572872 | tf_op jit(solution)/shard_map/ppermute | solution.py:871
  211.9 25.4 %collective-permute-start.25 = (bf16[10,2,2,2,32,128]{5,4,3,2,1,0:T(8,128)(2,1)S(1)}, bf16[10,2,2,2,32,128]{5,4,3,2,1,0:T(8,128)(2,1)S(1)}, u32[]{:S(2)}, u32[]{:S(2)}) collective-permute-start(bf16[10,2,2,2,32,128]{5,4,3,2,1,0:T(8,128)(2,1)S(1)} %dynamic-slice_bitcast_fusion.4), channel_id=1, source_target_pairs={{0,2},{1,3},{2,0},{3,1},{4,6},{5,7},{6,4},{7,5},{8,10},{9,11},{10,... | collective-permute-start | bytes 1966088 | tf_op jit(solution)/shard_map/ppermute | solution.py:871
  212.5 36.8 %collective-permute-start.33 = (bf16[2,8,64,1024]{3,2,1,0:T(8,128)(2,1)S(1)}, bf16[2,8,64,1024]{3,2,1,0:T(8,128)(2,1)S(1)}, u32[]{:S(2)}, u32[]{:S(2)}) collective-permute-start(bf16[2,8,64,1024]{3,2,1,0:T(8,128)(2,1)S(1)} %get-tuple-element.227), channel_id=1, source_target_pairs={{0,1},{1,0},{2,3},{3,2},{4,5},{5,4},{6,7},{7,6},{8,9},{9,8},{10,11... | collective-permute-start | bytes 6291464 | tf_op jit(solution)/shard_map/ppermute | solution.py:871
  222.5 20.4 %collective-permute-start.24 = (bf16[6,2,2,2,2,32,128]{6,5,4,3,2,1,0:T(8,128)(2,1)S(1)}, bf16[6,2,2,2,2,32,128]{6,5,4,3,2,1,0:T(8,128)(2,1)S(1)}, u32[]{:S(2)}, u32[]{:S(2)}) collective-permute-start(bf16[6,2,2,2,2,32,128]{6,5,4,3,2,1,0:T(8,128)(2,1)S(1)} %dynamic-slice_bitcast_fusion.2), channel_id=1, source_target_pairs={{0,4},{1,5},{2,6},{3,7},{4,0},{5,1},{6,2},{7,3},{8,12},{9,13},{10,... | collective-permute-start | bytes 2359304 | tf_op jit(solution)/shard_map/ppermute | solution.py:871
  223.9 20.2 %collective-permute-start.29 = (bf16[512,1024]{1,0:T(8,128)(2,1)S(1)}, bf16[512,1024]{1,0:T(8,128)(2,1)S(1)}, u32[]{:S(2)}, u32[]{:S(2)}) collective-permute-start(bf16[512,1024]{1,0:T(8,128)(2,1)S(1)} %get-tuple-element.218), channel_id=1, source_target_pairs={{0,1},{1,0},{2,3},{3,2},{4,5},{5,4},{6,7},{7,6},{8,9},{9,8},{10,11... | collective-permute-start | bytes 3145736 | tf_op jit(solution)/shard_map/ppermute | solution.py:871
  243.0 30.7 %collective-permute-start.35 = (bf16[16,2,64,128]{3,2,1,0:T(8,128)(2,1)S(1)}, bf16[16,2,64,128]{3,2,1,0:T(8,128)(2,1)S(1)}, u32[]{:S(2)}, u32[]{:S(2)}) collective-permute-start(bf16[16,2,64,128]{3,2,1,0:T(8,128)(2,1)S(1)} %maximum_select_fusion.8), channel_id=1, source_target_pairs={{0,8},{1,9},{2,10},{3,11},{4,12},{5,13},{6,14},{7,15},{8,0},{9,1},... | collective-permute-start | bytes 1572872 | tf_op jit(solution)/shard_map/ppermute | solution.py:871
  245.2 28.5 %collective-permute-start.36 = (bf16[6,2,2,2,32,128]{5,4,3,2,1,0:T(8,128)(2,1)S(1)}, bf16[6,2,2,2,32,128]{5,4,3,2,1,0:T(8,128)(2,1)S(1)}, u32[]{:S(2)}, u32[]{:S(2)}) collective-permute-start(bf16[6,2,2,2,32,128]{5,4,3,2,1,0:T(8,128)(2,1)S(1)} %dynamic-slice_bitcast_fusion.7), channel_id=1, source_target_pairs={{0,8},{1,9},{2,10},{3,11},{4,12},{5,13},{6,14},{7,15},{8,0},{9,1},... | collective-permute-start | bytes 1179656 | tf_op jit(solution)/shard_map/ppermute | solution.py:871
  250.4 27.1 %collective-permute-start.34 = (bf16[8,64,1024]{2,1,0:T(8,128)(2,1)S(1)}, bf16[8,64,1024]{2,1,0:T(8,128)(2,1)S(1)}, u32[]{:S(2)}, u32[]{:S(2)}) collective-permute-start(bf16[8,64,1024]{2,1,0:T(8,128)(2,1)S(1)} %slice_bitcast_fusion), channel_id=1, source_target_pairs={{0,2},{1,3},{2,0},{3,1},{4,6},{5,7},{6,4},{7,5},{8,10},{9,11},{10,... | collective-permute-start | bytes 3145736 | tf_op jit(solution)/shard_map/ppermute | solution.py:871
  252.3 29.4 %collective-permute-start.32 = (bf16[40,32,128]{2,1,0:T(8,128)(2,1)S(1)}, bf16[40,32,128]{2,1,0:T(8,128)(2,1)}, u32[]{:S(2)}, u32[]{:S(2)}) collective-permute-start(bf16[40,32,128]{2,1,0:T(8,128)(2,1)S(1)} %dynamic-slice_bitcast_fusion.8), channel_id=1, source_target_pairs={{0,16},{1,17},{2,18},{3,19},{4,20},{5,21},{6,22},{7,23},{8,24},{9,... | collective-permute-start | bytes 983048 | tf_op jit(solution)/shard_map/ppermute | solution.py:871
  275.1 33.0 %collective-permute-start.40 = (bf16[16,2,2,64,128]{4,3,2,1,0:T(8,128)(2,1)}, bf16[16,2,2,64,128]{4,3,2,1,0:T(8,128)(2,1)}, u32[]{:S(2)}, u32[]{:S(2)}) collective-permute-start(bf16[16,2,2,64,128]{4,3,2,1,0:T(8,128)(2,1)} %maximum_select_fusion.4), channel_id=1, source_target_pairs={{0,4},{1,5},{2,6},{3,7},{4,0},{5,1},{6,2},{7,3},{8,12},{9,13},{10,... | collective-permute-start | bytes 3145736 | tf_op jit(solution)/shard_map/ppermute | solution.py:871
  282.3 18.3 %all-to-all-start = ((f32[32,4,256]{2,1,0:T(4,128)}), f32[32,4,256]{2,1,0:T(4,128)S(1)}, u32[]{:S(2)}, u32[]{:S(2)}) async-start(f32[32,4,256]{2,1,0:T(4,128)} %bitcast.60), calls=%async_computation | async-start | bytes 262144 | tf_op jit(solution)/shard_map/all_to_all | solution.py:1167
  324.5 20.2 %collective-permute-start.42 = (bf16[40,2,32,128]{3,2,1,0:T(8,128)(2,1)S(1)}, bf16[40,2,32,128]{3,2,1,0:T(8,128)(2,1)S(1)}, u32[]{:S(2)}, u32[]{:S(2)}) collective-permute-start(bf16[40,2,32,128]{3,2,1,0:T(8,128)(2,1)S(1)} %maximum_select_fusion.7), channel_id=1, source_target_pairs={{0,4},{1,5},{2,6},{3,7},{4,0},{5,1},{6,2},{7,3},{8,12},{9,13},{10,... | collective-permute-start | bytes 1966088 | tf_op jit(solution)/shard_map/ppermute | solution.py:871
  345.4 30.8 %collective-permute-start.44 = (bf16[40,2,2,32,128]{4,3,2,1,0:T(8,128)(2,1)S(1)}, bf16[40,2,2,32,128]{4,3,2,1,0:T(8,128)(2,1)S(1)}, u32[]{:S(2)}, u32[]{:S(2)}) collective-permute-start(bf16[40,2,2,32,128]{4,3,2,1,0:T(8,128)(2,1)S(1)} %maximum_select_fusion.3), channel_id=1, source_target_pairs={{0,8},{1,9},{2,10},{3,11},{4,12},{5,13},{6,14},{7,15},{8,0},{9,1},... | collective-permute-start | bytes 3932168 | tf_op jit(solution)/shard_map/ppermute | solution.py:871
  345.7 19.5 %collective-permute-start.45 = (bf16[24,2,2,32,128]{4,3,0,1,2:T(8,128)(2,1)S(1)}, bf16[24,2,2,32,128]{4,3,0,1,2:T(8,128)(2,1)S(1)}, u32[]{:S(2)}, u32[]{:S(2)}) collective-permute-start(bf16[24,2,2,32,128]{4,3,0,1,2:T(8,128)(2,1)S(1)} %maximum_select_fusion.5), channel_id=1, source_target_pairs={{0,4},{1,5},{2,6},{3,7},{4,0},{5,1},{6,2},{7,3},{8,12},{9,13},{10,... | collective-permute-start | bytes 2359304 | tf_op jit(solution)/shard_map/ppermute | solution.py:871
  (50 other events, 539.0 us)
